TPU v7x, 32 devices: a whole 2x2x4 slice. The times are simulated.
32 devices in a mesh: dp: 8 (over y, x, core), mp: 4 (over z).
Axes of the slice: x: 2, y: 2, z: 4, core: 2. Of those that a mesh axis runs over, the one named last changes fastest.
Arguments:
- inputs: float32 [8192, 768], P(('dp', 'mp')), may hold values from -6 to 6
- cotangent: float32 [8192, 768], P(('dp', 'mp')), may hold values from -6 to 6
- mask_bits: int32 [8192], P(('dp', 'mp')), may hold values from 0 to 1, as said below
- frame_pregain: float32 [768], P(('dp', 'mp')), may hold values from 0.5 to 1.5
- frame_prebias: float32 [768], P(('dp', 'mp')), may hold values from -1.75 to 1.75
- frame_inweight: float32 [768, 3, 768], P('dp', None, 'mp'), may hold values from -0.21875 to 0.21875
- frame_inbias: float32 [2, 768], P(None, ('mp', 'dp')), may hold values from -1.75 to 1.75
- frame_outweight: float32 [768, 768], P('mp', 'dp'), may hold values from -0.875 to 0.875
- frame_outbias: float32 [768], P(('dp', 'mp')), may hold values from -1.75 to 1.75
- frame_midgain: float32 [768], P(('dp', 'mp')), may hold values from 0.5 to 1.5
- frame_midbias: float32 [768], P(('dp', 'mp')), may hold values from -1.75 to 1.75
- frame_upweight: float32 [768, 3072], P('dp', 'mp'), may hold values from -0.21875 to 0.21875
- frame_upbias: float32 [3072], P(('mp', 'dp')), may hold values from -1.75 to 1.75
- frame_downweight: float32 [3072, 768], P('mp', 'dp'), may hold values from -0.109375 to 0.109375
- frame_downbias: float32 [768], P(('dp', 'mp')), may hold values from -1.75 to 1.75
- tube_pregain: float32 [768], P(('dp', 'mp')), may hold values from 0.5 to 1.5
- tube_prebias: float32 [768], P(('dp', 'mp')), may hold values from -1.75 to 1.75
- tube_inweight: float32 [768, 3, 768], P('dp', None, 'mp'), may hold values from -0.21875 to 0.21875
- tube_inbias: float32 [2, 768], P(None, ('mp', 'dp')), may hold values from -1.75 to 1.75
- tube_outweight: float32 [768, 768], P('mp', 'dp'), may hold values from -0.875 to 0.875
- tube_outbias: float32 [768], P(('dp', 'mp')), may hold values from -1.75 to 1.75
- tube_midgain: float32 [768], P(('dp', 'mp')), may hold values from 0.5 to 1.5
- tube_midbias: float32 [768], P(('dp', 'mp')), may hold values from -1.75 to 1.75
- tube_upweight: float32 [768, 3072], P('dp', 'mp'), may hold values from -0.21875 to 0.21875
- tube_upbias: float32 [3072], P(('mp', 'dp')), may hold values from -1.75 to 1.75
- tube_downweight: float32 [3072, 768], P('mp', 'dp'), may hold values from -0.109375 to 0.109375
- tube_downbias: float32 [768], P(('dp', 'mp')), may hold values from -1.75 to 1.75
Outputs:
- outputs: float32 [8192, 768], P(('dp', 'mp'))
- input_grad: float32 [8192, 768], P(('dp', 'mp'))
- frame_pregain_grad: float32 [768], P(('dp', 'mp'))
- frame_prebias_grad: float32 [768], P(('dp', 'mp'))
- frame_inweight_grad: float32 [768, 3, 768], P('dp', None, 'mp')
- frame_inbias_grad: float32 [2, 768], P(None, ('mp', 'dp'))
- frame_outweight_grad: float32 [768, 768], P('mp', 'dp')
- frame_outbias_grad: float32 [768], P(('dp', 'mp'))
- frame_midgain_grad: float32 [768], P(('dp', 'mp'))
- frame_midbias_grad: float32 [768], P(('dp', 'mp'))
- frame_upweight_grad: float32 [768, 3072], P('dp', 'mp')
- frame_upbias_grad: float32 [3072], P(('mp', 'dp'))
- frame_downweight_grad: float32 [3072, 768], P('mp', 'dp')
- frame_downbias_grad: float32 [768], P(('dp', 'mp'))
- tube_pregain_grad: float32 [768], P(('dp', 'mp'))
- tube_prebias_grad: float32 [768], P(('dp', 'mp'))
- tube_inweight_grad: float32 [768, 3, 768], P('dp', None, 'mp')
- tube_inbias_grad: float32 [2, 768], P(None, ('mp', 'dp'))
- tube_outweight_grad: float32 [768, 768], P('mp', 'dp')
- tube_outbias_grad: float32 [768], P(('dp', 'mp'))
- tube_midgain_grad: float32 [768], P(('dp', 'mp'))
- tube_midbias_grad: float32 [768], P(('dp', 'mp'))
- tube_upweight_grad: float32 [768, 3072], P('dp', 'mp')
- tube_upbias_grad: float32 [3072], P(('mp', 'dp'))
- tube_downweight_grad: float32 [3072, 768], P('mp', 'dp')
- tube_downbias_grad: float32 [768], P(('dp', 'mp'))
Inputs may be any that keep to these rules, and one draw needn't show every extreme that they name: mask_bits is 0 or 1; each clip of 4096 tokens has its own masking probability, between one half and one.
All inputs are finite; a program needn't handle non-finite values.
Results may differ from a plain program's by a relative error of at most 0.02.
Values may be sent and summed in bfloat16 or wider, within the bound.
A program may use at most 192 MiB of HBM per device.

v0:
```python
import jax
import jax.numpy as jnp
from jax import lax
from jax.sharding import PartitionSpec as P

HEAD = 64
SIDE = 16
TUBE = 4
SPLIT = 4


EPS = 1e-06


def from_partner(value, axis, bit):
    mask = 2**bit
    pairs = [(source, source ^ mask) for source in range(lax.axis_size(axis))]
    return lax.ppermute(value, axis, pairs)


def norm_rows(values, gain, shift):
    center = values - jnp.mean(values, axis=-1, keepdims=True)
    spread = jnp.mean(center * center, axis=-1, keepdims=True)
    return center * lax.rsqrt(spread + EPS) * gain + shift


def gelu_exact(values):
    return jax.nn.gelu(values, approximate=False)


def spatial_split(rows):
    return rows.reshape(rows.shape[0] // (SIDE * SIDE), SIDE * SIDE, rows.shape[-1])


def spatial_join(windows):
    return windows.reshape(-1, windows.shape[-1])


def tube_split(rows):
    frames = rows.shape[0] // (SIDE * SIDE)
    across = SIDE // TUBE
    width = rows.shape[-1]
    shaped = rows.reshape(frames, across, TUBE, across, TUBE, width).transpose(1, 3, 0, 2, 4, 5)
    return shaped.reshape(across * across, frames * TUBE * TUBE, width)


def tube_join(windows):
    across = SIDE // TUBE
    frames = windows.shape[1] // (TUBE * TUBE)
    width = windows.shape[-1]
    shaped = windows.reshape(across, across, frames, TUBE, TUBE, width).transpose(2, 0, 3, 1, 4, 5)
    return shaped.reshape(-1, width)


def inner(left, right):
    return lax.dot_general(
        left, right, (((0,), (0,)), ((), ())), preferred_element_type=jnp.float32
    )


def against(left, weight):
    return lax.dot_general(
        left, weight, (((1,), (1,)), ((), ())), preferred_element_type=jnp.float32
    )


def fetch(params):
    (
        pregain,
        prebias,
        inweight,
        inbias,
        outweight,
        outbias,
        midgain,
        midbias,
        upweight,
        upbias,
        downweight,
        downbias,
    ) = params
    half = jnp.bfloat16
    large = (
        lax.all_gather(inweight.astype(half), "dp", axis=0, tiled=True),
        lax.all_gather(inbias.astype(half), "dp", axis=1, tiled=True),
        lax.all_gather(outweight.astype(half), "dp", axis=1, tiled=True),
        lax.all_gather(upweight.astype(half), "dp", axis=0, tiled=True),
        lax.all_gather(upbias.astype(half), "dp", axis=0, tiled=True),
        lax.all_gather(downweight.astype(half), "dp", axis=1, tiled=True),
    )
    small = (
        lax.all_gather(pregain.astype(half), ("dp", "mp"), axis=0, tiled=True),
        lax.all_gather(prebias.astype(half), ("dp", "mp"), axis=0, tiled=True),
        lax.all_gather(outbias.astype(half), ("dp", "mp"), axis=0, tiled=True),
        lax.all_gather(midgain.astype(half), ("dp", "mp"), axis=0, tiled=True),
        lax.all_gather(midbias.astype(half), ("dp", "mp"), axis=0, tiled=True),
        lax.all_gather(downbias.astype(half), ("dp", "mp"), axis=0, tiled=True),
    )
    return (large, tuple((entry.astype(jnp.float32) for entry in small)))


def share_rows(values):
    return lax.all_gather(values, "mp", axis=0, tiled=True)


def share_grads(values):
    return lax.all_gather(values, "mp", axis=0, tiled=True)


def reduce_rows(values, weight):
    return lax.psum_scatter(
        jnp.dot(values, weight, preferred_element_type=jnp.float32).astype(jnp.bfloat16),
        "mp",
        scatter_dimension=0,
        tiled=True,
    ).astype(jnp.float32)


def back_rows(apply, rows):
    return lax.psum_scatter(
        apply(jnp.int32(0), lax.axis_size("mp") * rows).astype(jnp.bfloat16),
        "mp",
        scatter_dimension=0,
        tiled=True,
    ).astype(jnp.float32)


def share_keys(pairs):
    place = lax.axis_index("dp")
    for bit in range(SPLIT.bit_length() - 1):
        other = from_partner(pairs, "dp", bit)
        upper = place >> bit & 1 == 1
        pairs = jnp.where(
            upper, jnp.concatenate([other, pairs], axis=2), jnp.concatenate([pairs, other], axis=2)
        )
    return pairs


def return_keys(pairs):
    place = lax.axis_index("dp")
    for bit in reversed(range(SPLIT.bit_length() - 1)):
        half = pairs.shape[2] // 2
        lower_part = pairs[:, :, :half]
        upper_part = pairs[:, :, half:]
        upper = place >> bit & 1 == 1
        keep = jnp.where(upper, upper_part, lower_part)
        send = jnp.where(upper, lower_part, upper_part)
        pairs = keep + from_partner(send.astype(jnp.bfloat16), "dp", bit).astype(send.dtype)
    return pairs


def plain_rows(packed, split, tubular):
    queries = split(packed[:, 0])
    pairs = jnp.stack([split(packed[:, 1]), split(packed[:, 2])])
    if tubular:
        pairs = share_keys(pairs)
    return (queries, pairs[0], pairs[1])


def plain_return(query_grad, key_grad, value_grad, join, tubular):
    windows, qlength, heads, head_size = query_grad.shape
    width = heads * head_size
    keylen = key_grad.shape[1]
    pair_grad = jnp.stack(
        [key_grad.reshape(windows, keylen, width), value_grad.reshape(windows, keylen, width)]
    )
    if tubular:
        pair_grad = return_keys(pair_grad)
    return jnp.stack(
        [join(query_grad.reshape(windows, qlength, width)), join(pair_grad[0]), join(pair_grad[1])],
        axis=1,
    ).astype(jnp.bfloat16)


def arrangement(tubular):
    if tubular:
        return (tube_split, tube_join)
    return (spatial_split, spatial_join)


def forward(start_rows, large, small, tubular):
    inweight, inbias, outweight, upweight, upbias, downweight = large
    pregain, prebias, outbias, midgain, midbias, downbias = small
    split, join = arrangement(tubular)
    normed_all = share_rows(norm_rows(start_rows, pregain, prebias).astype(jnp.bfloat16))
    width = inweight.shape[2]
    count = normed_all.shape[0]
    pre = jnp.dot(
        normed_all,
        inweight.reshape(inweight.shape[0], 3 * width),
        preferred_element_type=jnp.float32,
    ).reshape(count, 3, width)
    offset = jnp.stack(
        [
            inbias[0].astype(jnp.float32),
            jnp.zeros((width,), jnp.float32),
            inbias[1].astype(jnp.float32),
        ]
    )
    packed = (pre + offset).astype(jnp.bfloat16)
    query_rows, key_rows, value_rows = plain_rows(packed, split, tubular)
    heads = width // HEAD
    windows = query_rows.shape[0]
    qlength = query_rows.shape[1]
    keylen = key_rows.shape[1]
    query_heads = query_rows.reshape(windows, qlength, heads, HEAD)
    key_heads = key_rows.reshape(windows, keylen, heads, HEAD)
    value_heads = value_rows.reshape(windows, keylen, heads, HEAD)
    scale = HEAD ** (-0.5)
    scores = (
        jnp.einsum("wqhd,wkhd->whqk", query_heads, key_heads, preferred_element_type=jnp.float32)
        * scale
    )
    highest = jnp.max(scores, axis=-1, keepdims=True)
    expo = jnp.exp(scores - highest)
    total = jnp.sum(expo, axis=-1, keepdims=True)
    probs = expo / total
    logsum = highest + jnp.log(total)
    mixed = jnp.einsum(
        "whqk,wkhd->wqhd",
        probs.astype(jnp.bfloat16),
        value_heads,
        preferred_element_type=jnp.float32,
    )
    window_context = mixed.reshape(windows, qlength, width).astype(jnp.bfloat16)
    context = join(window_context)
    middle = start_rows + reduce_rows(context, outweight) + outbias
    normed_next = share_rows(norm_rows(middle, midgain, midbias).astype(jnp.bfloat16))
    upper = jnp.dot(normed_next, upweight, preferred_element_type=jnp.float32) + upbias.astype(
        jnp.float32
    )
    hidden = gelu_exact(upper).astype(jnp.bfloat16)
    result = middle + reduce_rows(hidden, downweight) + downbias
    kept = (
        start_rows,
        normed_all,
        query_heads,
        key_heads,
        value_heads,
        logsum,
        context,
        middle,
        normed_next,
        upper,
        hidden,
    )
    return (result, kept)


def backward(grad, kept, large, small, tubular):
    inweight, inbias, outweight, upweight, upbias, downweight = large
    pregain, prebias, outbias, midgain, midbias, downbias = small
    (
        start_rows,
        normed_all,
        query_heads,
        key_heads,
        value_heads,
        logsum,
        context,
        middle,
        normed_next,
        upper,
        hidden,
    ) = kept
    split, join = arrangement(tubular)
    rows = grad.shape[0]
    downbias_grad = jnp.sum(grad, axis=0)
    grad_all = share_grads(grad.astype(jnp.bfloat16))
    downweight_grad = inner(hidden, grad_all)
    hidden_grad = against(grad_all, downweight)
    gelu_back = jax.vjp(gelu_exact, upper)[1]
    upper_grad = gelu_back(hidden_grad)[0].astype(jnp.bfloat16)
    upbias_grad = jnp.sum(upper_grad.astype(jnp.float32), axis=0)
    upweight_grad = inner(normed_next, upper_grad)

    def up_term(start, count):
        return against(upper_grad, upweight)

    second_grad = back_rows(up_term, rows)
    middle_back = jax.vjp(norm_rows, middle, midgain, midbias)[1]
    middle_part, midgain_grad, midbias_grad = middle_back(second_grad)
    middle_grad = grad + middle_part
    outbias_grad = jnp.sum(middle_grad, axis=0)
    middle_all = share_grads(middle_grad.astype(jnp.bfloat16))
    outweight_grad = inner(context, middle_all)
    context_grad = against(middle_all, outweight).astype(jnp.bfloat16)
    window_grad = split(context_grad)
    context_heads = window_grad.reshape(query_heads.shape)
    scale = HEAD ** (-0.5)
    scores = (
        jnp.einsum("wqhd,wkhd->whqk", query_heads, key_heads, preferred_element_type=jnp.float32)
        * scale
    )
    probs = jnp.exp(scores - logsum)
    prob_grad = jnp.einsum(
        "wqhd,wkhd->whqk", context_heads, value_heads, preferred_element_type=jnp.float32
    )
    score_grad = (probs * (prob_grad - jnp.sum(probs * prob_grad, axis=-1, keepdims=True))).astype(
        jnp.bfloat16
    )
    query_grad = (
        jnp.einsum("whqk,wkhd->wqhd", score_grad, key_heads, preferred_element_type=jnp.float32)
        * scale
    )
    key_grad = (
        jnp.einsum("whqk,wqhd->wkhd", score_grad, query_heads, preferred_element_type=jnp.float32)
        * scale
    )
    value_grad = jnp.einsum(
        "whqk,wqhd->wkhd",
        probs.astype(jnp.bfloat16),
        context_heads,
        preferred_element_type=jnp.float32,
    )
    packed_grad = plain_return(query_grad, key_grad, value_grad, join, tubular)
    inbias_grad = jnp.stack(
        [
            jnp.sum(packed_grad[:, 0].astype(jnp.float32), axis=0),
            jnp.sum(packed_grad[:, 2].astype(jnp.float32), axis=0),
        ]
    )
    inweight_grad = jnp.einsum(
        "gd,gtc->dtc", normed_all, packed_grad, preferred_element_type=jnp.float32
    )

    def in_term(start, count):
        return jnp.einsum("gtc,dtc->gd", packed_grad, inweight, preferred_element_type=jnp.float32)

    first_grad = back_rows(in_term, rows)
    first_back = jax.vjp(norm_rows, start_rows, pregain, prebias)[1]
    input_part, pregain_grad, prebias_grad = first_back(first_grad)
    large_grads = (
        inweight_grad,
        inbias_grad,
        outweight_grad,
        upweight_grad,
        upbias_grad,
        downweight_grad,
    )
    small_grads = (
        pregain_grad,
        prebias_grad,
        outbias_grad,
        midgain_grad,
        midbias_grad,
        downbias_grad,
    )
    return (middle_grad + input_part, large_grads, small_grads)


def settle(large, small):
    large = (
        lax.psum_scatter(large[0], "dp", scatter_dimension=0, tiled=True),
        lax.psum_scatter(large[1], "dp", scatter_dimension=1, tiled=True),
        lax.psum_scatter(large[2], "dp", scatter_dimension=1, tiled=True),
        lax.psum_scatter(large[3], "dp", scatter_dimension=0, tiled=True),
        lax.psum_scatter(large[4], "dp", scatter_dimension=0, tiled=True),
        lax.psum_scatter(large[5], "dp", scatter_dimension=1, tiled=True),
    )
    small = (
        lax.psum_scatter(small[0], ("dp", "mp"), scatter_dimension=0, tiled=True),
        lax.psum_scatter(small[1], ("dp", "mp"), scatter_dimension=0, tiled=True),
        lax.psum_scatter(small[2], ("dp", "mp"), scatter_dimension=0, tiled=True),
        lax.psum_scatter(small[3], ("dp", "mp"), scatter_dimension=0, tiled=True),
        lax.psum_scatter(small[4], ("dp", "mp"), scatter_dimension=0, tiled=True),
        lax.psum_scatter(small[5], ("dp", "mp"), scatter_dimension=0, tiled=True),
    )
    return (large, small)


def arrange(large, small):
    return (
        small[0],
        small[1],
        large[0],
        large[1],
        large[2],
        small[2],
        small[3],
        small[4],
        large[3],
        large[4],
        large[5],
        small[5],
    )


def shards(
    inputs,
    cotangent,
    mask_bits,
    frame_pregain,
    frame_prebias,
    frame_inweight,
    frame_inbias,
    frame_outweight,
    frame_outbias,
    frame_midgain,
    frame_midbias,
    frame_upweight,
    frame_upbias,
    frame_downweight,
    frame_downbias,
    tube_pregain,
    tube_prebias,
    tube_inweight,
    tube_inbias,
    tube_outweight,
    tube_outbias,
    tube_midgain,
    tube_midbias,
    tube_upweight,
    tube_upbias,
    tube_downweight,
    tube_downbias,
):
    frame_large, frame_small = fetch(
        (
            frame_pregain,
            frame_prebias,
            frame_inweight,
            frame_inbias,
            frame_outweight,
            frame_outbias,
            frame_midgain,
            frame_midbias,
            frame_upweight,
            frame_upbias,
            frame_downweight,
            frame_downbias,
        )
    )
    middle, frame_kept = forward(inputs, frame_large, frame_small, False)
    tube_large, tube_small = fetch(
        (
            tube_pregain,
            tube_prebias,
            tube_inweight,
            tube_inbias,
            tube_outweight,
            tube_outbias,
            tube_midgain,
            tube_midbias,
            tube_upweight,
            tube_upbias,
            tube_downweight,
            tube_downbias,
        )
    )
    result, tube_kept = forward(middle, tube_large, tube_small, True)
    grad = cotangent * mask_bits.astype(jnp.float32)[:, None]
    grad, tube_big, tube_row = backward(grad, tube_kept, tube_large, tube_small, True)
    tube_big, tube_row = settle(tube_big, tube_row)
    grad, frame_big, frame_row = backward(grad, frame_kept, frame_large, frame_small, False)
    frame_big, frame_row = settle(frame_big, frame_row)
    return (result, grad) + arrange(frame_big, frame_row) + arrange(tube_big, tube_row)


def solution(mesh):
    return jax.shard_map(
        shards,
        mesh=mesh,
        in_specs=(
            P(("dp", "mp"), None),
            P(("dp", "mp"), None),
            P(("dp", "mp")),
            P(("dp", "mp")),
            P(("dp", "mp")),
            P("dp", None, "mp"),
            P(None, ("mp", "dp")),
            P("mp", "dp"),
            P(("dp", "mp")),
            P(("dp", "mp")),
            P(("dp", "mp")),
            P("dp", "mp"),
            P(("mp", "dp")),
            P("mp", "dp"),
            P(("dp", "mp")),
            P(("dp", "mp")),
            P(("dp", "mp")),
            P("dp", None, "mp"),
            P(None, ("mp", "dp")),
            P("mp", "dp"),
            P(("dp", "mp")),
            P(("dp", "mp")),
            P(("dp", "mp")),
            P("dp", "mp"),
            P(("mp", "dp")),
            P("mp", "dp"),
            P(("dp", "mp")),
        ),
        out_specs=(
            P(("dp", "mp"), None),
            P(("dp", "mp"), None),
            P(("dp", "mp")),
            P(("dp", "mp")),
            P("dp", None, "mp"),
            P(None, ("mp", "dp")),
            P("mp", "dp"),
            P(("dp", "mp")),
            P(("dp", "mp")),
            P(("dp", "mp")),
            P("dp", "mp"),
            P(("mp", "dp")),
            P("mp", "dp"),
            P(("dp", "mp")),
            P(("dp", "mp")),
            P(("dp", "mp")),
            P("dp", None, "mp"),
            P(None, ("mp", "dp")),
            P("mp", "dp"),
            P(("dp", "mp")),
            P(("dp", "mp")),
            P(("dp", "mp")),
            P("dp", "mp"),
            P(("mp", "dp")),
            P("mp", "dp"),
            P(("dp", "mp")),
        ),
        check_vma=False,
    )
```

profile of v0, /device:TPU:0, one launch (start us, length us, event | category | flops | bytes accessed | tf_op | source)
XLA Modules:
  0.0 1390.2 jit_solution(122292402366063408)
XLA Ops:
  21.3 42.7 %all-reduce.32 = (bf16[768]{0:T(1024)(128)(2,1)S(1)}, bf16[768]{0:T(1024)(128)(2,1)S(1)}, bf16[768]{0:T(1024)(128)(2,1)S(1)}, bf16[768]{0:T(1024)(128)(2,1)S(1)}...) all-reduce(bf16[768]{0:T(1024)(128)(2,1)S(1)} %dynamic-update-slice, ...), channel_id=1, replica_groups=mesh['dp'=8,'mp'=4] {'dp','mp'}, use_global_device_ids=true, to_apply=%add.1 | all-reduce | flops 9216 | bytes 36864
  66.1 9.8 all-gather.1
  76.0 7.8 all-gather
  84.1 11.9 all_gather.99
  96.7 8.6 all_gather.101
  120.1 32.2 %reduce-scatter.23.cloned.1.call-done = bf16[256,768]{1,0:T(8,128)(2,1)} async-done(((bf16[1024,768]{1,0:T(8,128)(2,1)}), bf16[256,768]{1,0:T(8,128)(2,1)}) %reduce-scatter.23.cloned.1.call-update) | async-done | bytes 393232 | tf_op jit(solution)/shard_map/reduce_scatter | solution.py:111
  163.9 15.0 %all-reduce.33 = (bf16[768]{0:T(1024)(128)(2,1)}, bf16[768]{0:T(1024)(128)(2,1)}) all-reduce(bf16[768]{0:T(1024)(128)(2,1)} %dynamic-update-slice.5, bf16[768]{0:T(1024)(128)(2,1)S(1)} %dynamic-update-slice.12), channel_id=1, replica_groups=mesh['dp'=8,'mp'=4] {'dp'}, use_global_device_ids=true, to_apply=%add.5 | all-reduce | flops 1536 | bytes 6144
  179.6 12.1 all-gather.17.cloned.1.call-done
  191.6 11.1 multiply_convert_fusion.3
  202.8 14.0 %all-gather.21.cloned.1.call-done = bf16[768,768]{0,1:T(8,128)(2,1)} async-done(((bf16[768,96]{0,1:T(8,128)(2,1)}), bf16[768,768]{0,1:T(8,128)(2,1)}) %all-gather.21.cloned.1.call-update) | async-done | bytes 1179664 | tf_op jit(solution)/shard_map/all_gather | solution.py:89
  216.7 4.4 convolution_convert_fusion.4
  223.2 33.4 %reduce-scatter.25.cloned.1.call-done = bf16[256,768]{1,0:T(8,128)(2,1)} async-done(((bf16[1024,768]{1,0:T(8,128)(2,1)}), bf16[256,768]{1,0:T(8,128)(2,1)}) %reduce-scatter.25.cloned.1.call-update) | async-done | bytes 393232 | tf_op jit(solution)/shard_map/reduce_scatter | solution.py:111
  262.2 12.4 all_gather.113
  277.0 20.2 %all-gather.23.cloned.1.call-done = bf16[1024,768]{1,0:T(8,128)(2,1)} async-done(((bf16[256,768]{1,0:T(8,128)(2,1)}), bf16[1024,768]{1,0:T(8,128)(2,1)}) %all-gather.23.cloned.1.call-update) | async-done | bytes 1572880 | tf_op jit(solution)/shard_map/all_gather | solution.py:103
  324.3 4.5 maximum_select_fusion.1
  335.7 39.3 %all_gather.115 = bf16[192,768]{0,1:T(8,128)(2,1)} all-gather(bf16[192,96]{0,1:T(8,128)(2,1)} %copy.304), channel_id=1, replica_groups=mesh['dp'=8,'mp'=4] {'dp'}, dimensions={1}, use_global_device_ids=true | all-gather | bytes 331776 | tf_op jit(solution)/shard_map/all_gather | solution.py:86
  390.2 5.0 maximum_select_fusion
  430.1 28.5 %reduce-scatter.27.cloned.1.call-done = bf16[256,768]{1,0:T(8,128)(2,1)} async-done(((bf16[1024,768]{1,0:T(8,128)(2,1)}), bf16[256,768]{1,0:T(8,128)(2,1)}) %reduce-scatter.27.cloned.1.call-update) | async-done | bytes 393232 | tf_op jit(solution)/shard_map/reduce_scatter | solution.py:111
  469.7 29.4 %all-gather.25.cloned.1.call-done = bf16[1024,768]{1,0:T(8,128)(2,1)} async-done(((bf16[256,768]{1,0:T(8,128)(2,1)}), bf16[1024,768]{1,0:T(8,128)(2,1)}) %all-gather.25.cloned.1.call-update) | async-done | bytes 1572880 | tf_op jit(solution)/shard_map/all_gather | solution.py:103
  499.1 4.7 fusion.103
  503.8 20.4 %all-gather.29.cloned.1.call-done = bf16[768,768]{0,1:T(8,128)(2,1)} async-done(((bf16[768,96]{0,1:T(8,128)(2,1)}), bf16[768,768]{0,1:T(8,128)(2,1)}) %all-gather.29.cloned.1.call-update) | async-done | bytes 1179664 | tf_op jit(solution)/shard_map/all_gather | solution.py:89
  524.2 38.4 %all-gather.31.cloned.1.call-done = bf16[1024,768]{1,0:T(8,128)(2,1)} async-done(((bf16[256,768]{1,0:T(8,128)(2,1)}), bf16[1024,768]{1,0:T(8,128)(2,1)}) %all-gather.31.cloned.1.call-update) | async-done | bytes 1572880 | tf_op jit(solution)/shard_map/all_gather | solution.py:107
  562.6 12.2 convert_reduce_fusion
  587.1 25.8 %reduce-scatter.31.cloned.1.call-done = bf16[256,768]{1,0:T(8,128)(2,1)} async-done(((bf16[1024,768]{1,0:T(8,128)(2,1)}), bf16[256,768]{1,0:T(8,128)(2,1)}) %reduce-scatter.31.cloned.1.call-update) | async-done | bytes 393232 | tf_op jit(solution)/shard_map/reduce_scatter | solution.py:120
  619.1 30.2 %reduce-scatter.29.cloned.1.call-done = bf16[256,768]{1,0:T(8,128)(2,1)} async-done(((bf16[1024,768]{1,0:T(8,128)(2,1)}), bf16[256,768]{1,0:T(8,128)(2,1)}) %reduce-scatter.29.cloned.1.call-update) | async-done | bytes 393232 | tf_op jit(solution)/shard_map/reduce_scatter | solution.py:111
  656.4 34.1 %all-gather.33.cloned.1.call-done = bf16[1024,768]{1,0:T(8,128)(2,1)} async-done(((bf16[256,768]{1,0:T(8,128)(2,1)}), bf16[1024,768]{1,0:T(8,128)(2,1)}) %all-gather.33.cloned.1.call-update) | async-done | bytes 1572880 | tf_op jit(solution)/shard_map/all_gather | solution.py:107
  705.0 4.3 multiply_reduce_fusion.1
  716.1 4.9 copy.312
  721.0 4.9 copy.313
  725.9 4.7 select_convert_fusion
  736.0 34.6 %collective-permute-done.2 = bf16[2,16,128,192]{2,3,1,0:T(8,128)(2,1)} collective-permute-done((bf16[2,16,128,192]{2,3,1,0:T(8,128)(2,1)}, bf16[2,16,128,192]{2,3,1,0:T(8,128)(2,1)}, u32[]{:S(2)}, u32[]{:S(2)}) %collective-permute-start.2) | collective-permute-done | bytes 1572896 | tf_op jit(solution)/shard_map/ppermute | solution.py:18
  774.4 4.4 convert_add_fusion
  821.7 34.8 %reduce-scatter.33.cloned.1.call-done = bf16[256,768]{1,0:T(8,128)(2,1)} async-done(((bf16[1024,768]{1,0:T(8,128)(2,1)}), bf16[256,768]{1,0:T(8,128)(2,1)}) %reduce-scatter.33.cloned.1.call-update) | async-done | bytes 393232 | tf_op jit(solution)/shard_map/reduce_scatter | solution.py:120
  865.8 36.0 %all-gather.35.cloned.1.call-done = bf16[1024,768]{1,0:T(8,128)(2,1)} async-done(((bf16[256,768]{1,0:T(8,128)(2,1)}), bf16[1024,768]{1,0:T(8,128)(2,1)}) %all-gather.35.cloned.1.call-update) | async-done | bytes 1572880 | tf_op jit(solution)/shard_map/all_gather | solution.py:107
  901.7 6.5 convert_reduce_fusion.1
  912.1 34.2 %reduce-scatter.35.cloned.1.call-done = bf16[256,768]{1,0:T(8,128)(2,1)} async-done(((bf16[1024,768]{1,0:T(8,128)(2,1)}), bf16[256,768]{1,0:T(8,128)(2,1)}) %reduce-scatter.35.cloned.1.call-update) | async-done | bytes 393232 | tf_op jit(solution)/shard_map/reduce_scatter | solution.py:120
  959.8 31.7 %all-gather.37.cloned.1.call-done = bf16[1024,768]{1,0:T(8,128)(2,1)} async-done(((bf16[256,768]{1,0:T(8,128)(2,1)}), bf16[1024,768]{1,0:T(8,128)(2,1)}) %all-gather.37.cloned.1.call-update) | async-done | bytes 1572880 | tf_op jit(solution)/shard_map/all_gather | solution.py:107
  1023.0 5.0 fusion.106
  1031.3 4.9 fusion.105
  1036.2 4.4 fusion.104
  1048.9 23.7 %all-reduce.31 = (f32[2,192]{1,0:T(2,128)S(1)}, f32[768]{0:T(1024)S(1)}, f32[2,192]{1,0:T(2,128)S(1)}, f32[768]{0:T(1024)S(1)}) all-reduce(f32[2,192]{1,0:T(2,128)S(1)} %pad_maximum_fusion.6, f32[768]{0:T(1024)S(1)} %copy-done.74, f32[2,192]{1,0:T(2,128)S(1)} %pad_maximum_fusion.7, ...), channel_id=13, replica_groups=mesh['dp'=8,'mp'=4] {'dp'}, use_global_device_ids=true, to_apply=%region_37.38.clone | all-reduce | flops 2304 | bytes 18432
  1076.6 27.8 %reduce-scatter.37.cloned.1.call-done = bf16[256,768]{1,0:T(8,128)(2,1)} async-done(((bf16[1024,768]{1,0:T(8,128)(2,1)}), bf16[256,768]{1,0:T(8,128)(2,1)}) %reduce-scatter.37.cloned.1.call-update) | async-done | bytes 393232 | tf_op jit(solution)/shard_map/reduce_scatter | solution.py:120
  1107.3 40.1 %all-reduce.30 = (f32[768]{0:T(1024)S(1)}, f32[768]{0:T(1024)S(1)}, f32[768]{0:T(1024)S(1)}, f32[768]{0:T(1024)S(1)}, f32[768]{0:T(1024)S(1)}, /*index=5*/f32[76...) all-reduce(f32[768]{0:T(1024)S(1)} %get-tuple-element.32, ...), channel_id=10, replica_groups=mesh['dp'=8,'mp'=4] {'dp','mp'}, use_global_device_ids=true, to_apply=%region_31.32.clone | all-reduce | flops 9216 | bytes 73728
  1156.6 39.9 %reduce-scatter.47.cloned.1.call-done = f32[96,768]{1,0:T(8,128)} async-done(((f32[768,768]{1,0:T(8,128)}), f32[96,768]{1,0:T(8,128)}) %reduce-scatter.47.cloned.1.call-update) | async-done | bytes 294928 | tf_op jit(solution)/shard_map/reduce_scatter | solution.py:357
  1196.5 46.3 %reduce-scatter.45.cloned.1.call-done = f32[96,3,192]{2,0,1:T(8,128)} async-done(((f32[768,3,192]{2,0,1:T(8,128)}), f32[96,3,192]{2,0,1:T(8,128)}) %reduce-scatter.45.cloned.1.call-update) | async-done | bytes 221200 | tf_op jit(solution)/shard_map/reduce_scatter | solution.py:354
  1242.8 46.6 %reduce-scatter.43.cloned.1.call-done = f32[768,96]{0,1:T(8,128)} async-done(((f32[768,768]{0,1:T(8,128)}), f32[768,96]{0,1:T(8,128)}) %reduce-scatter.43.cloned.1.call-update) | async-done | bytes 294928 | tf_op jit(solution)/shard_map/reduce_scatter | solution.py:359
  1289.5 46.2 %reduce-scatter.41.cloned.1.call-done = f32[96,768]{1,0:T(8,128)} async-done(((f32[768,768]{1,0:T(8,128)}), f32[96,768]{1,0:T(8,128)}) %reduce-scatter.41.cloned.1.call-update) | async-done | bytes 294928 | tf_op jit(solution)/shard_map/reduce_scatter | solution.py:357
  1335.6 46.7 %reduce-scatter.39.cloned.1.call-done = f32[96,3,192]{2,0,1:T(8,128)} async-done(((f32[768,3,192]{2,0,1:T(8,128)}), f32[96,3,192]{2,0,1:T(8,128)}) %reduce-scatter.39.cloned.1.call-update) | async-done | bytes 221200 | tf_op jit(solution)/shard_map/reduce_scatter | solution.py:354
  (484 shorter events, 330.0 us)
Async XLA Ops:
  8.0 68.0 %copy-start.83 = (f32[2,24]{1,0:T(2,128)S(1)}, f32[2,24]{1,0:T(2,128)}, u32[]{:S(2)}) copy-start(f32[2,24]{1,0:T(2,128)} %param.33) | copy-start | bytes 580
  8.1 75.8 %copy-start.43 = (f32[192,96]{1,0:T(8,128)S(1)}, f32[192,96]{1,0:T(8,128)}, u32[]{:S(2)}) copy-start(f32[192,96]{1,0:T(8,128)} %param.34) | copy-start | bytes 221188
  8.1 76.0 %copy-start.36 = (f32[96,3,192]{2,0,1:T(8,128)S(1)}, f32[96,3,192]{2,0,1:T(8,128)}, u32[]{:S(2)}) copy-start(f32[96,3,192]{2,0,1:T(8,128)} %param.32) | copy-start | bytes 663556
  8.1 97.9 %all-gather.15.cloned.1.call-start = ((), (), s32[]{:S(2)}) async-start(), calls=%async_computation.16 | async-start | bytes 1966080 | tf_op jit(solution)/shard_map/all_gather | solution.py:103
  17.3 79.3 %copy-start.45 = (f32[256]{0:T(256)}, f32[256]{0:T(256)S(1)}, u32[]{:S(2)}) copy-start(f32[256]{0:T(256)S(1)} %broadcast_multiply_fusion.3) | copy-start | bytes 3076
  18.7 87.2 %copy-start.50 = (f32[256]{0:T(256)}, f32[256]{0:T(256)S(1)}, u32[]{:S(2)}) copy-start(f32[256]{0:T(256)S(1)} %fusion.76) | copy-start | bytes 3076
  66.0 86.3 %reduce-scatter.23.cloned.1.call-start = ((), (), s32[]{:S(2)}) async-start(), calls=%async_computation.17 | async-start | bytes 1966080 | tf_op jit(solution)/shard_map/reduce_scatter | solution.py:111
  117.8 61.8 %all-gather.19.cloned.1.call-start = ((), (), s32[]{:S(2)}) async-start(), calls=%async_computation.19 | async-start | bytes 1327104 | tf_op jit(solution)/shard_map/all_gather | solution.py:87
  119.5 72.1 %all-gather.17.cloned.1.call-start = ((), (), s32[]{:S(2)}) async-start(), calls=%async_computation.18 | async-start | bytes 1966080 | tf_op jit(solution)/shard_map/all_gather | solution.py:103
  155.6 61.2 %all-gather.21.cloned.1.call-start = ((), (), s32[]{:S(2)}) async-start(), calls=%async_computation.20 | async-start | bytes 1327104 | tf_op jit(solution)/shard_map/all_gather | solution.py:89
  157.3 99.3 %reduce-scatter.25.cloned.1.call-start = ((), (), s32[]{:S(2)}) async-start(), calls=%async_computation.21 | async-start | bytes 1966080 | tf_op jit(solution)/shard_map/reduce_scatter | solution.py:111
  221.2 76.0 %all-gather.23.cloned.1.call-start = ((), (), s32[]{:S(2)}) async-start(), calls=%async_computation.22 | async-start | bytes 1966080 | tf_op jit(solution)/shard_map/all_gather | solution.py:103
  261.2 197.4 %reduce-scatter.27.cloned.1.call-start = ((), (), s32[]{:S(2)}) async-start(), calls=%async_computation.23 | async-start | bytes 1966080 | tf_op jit(solution)/shard_map/reduce_scatter | solution.py:111
  321.3 3.0 collective-permute-start
  332.6 53.8 %collective-permute-start.1 = (bf16[2,16,128,192]{2,3,1,0:T(8,128)(2,1)}, bf16[2,16,128,192]{2,3,1,0:T(8,128)(2,1)}, u32[]{:S(2)}, u32[]{:S(2)}) collective-permute-start(bf16[2,16,128,192]{2,3,1,0:T(8,128)(2,1)} %copy.294), channel_id=1, source_target_pairs={{0,8},{4,12},{8,0},{12,4},{16,24},{20,28},{24,16},{28,20},{1,9},{5... | collective-permute-start | bytes 4718600 | tf_op jit(solution)/shard_map/ppermute | solution.py:18
  425.1 44.6 %all-gather.27.cloned.1.call-start = ((), (), s32[]{:S(2)}) async-start(), calls=%async_computation.25 | async-start | bytes 1327104 | tf_op jit(solution)/shard_map/all_gather | solution.py:87
  426.8 72.3 %all-gather.25.cloned.1.call-start = ((), (), s32[]{:S(2)}) async-start(), calls=%async_computation.24 | async-start | bytes 1966080 | tf_op jit(solution)/shard_map/all_gather | solution.py:103
  463.1 61.1 %all-gather.29.cloned.1.call-start = ((), (), s32[]{:S(2)}) async-start(), calls=%async_computation.26 | async-start | bytes 1327104 | tf_op jit(solution)/shard_map/all_gather | solution.py:89
  464.8 97.8 %all-gather.31.cloned.1.call-start = ((), (), s32[]{:S(2)}) async-start(), calls=%async_computation.28 | async-start | bytes 1966080 | tf_op jit(solution)/shard_map/all_gather | solution.py:107
  468.1 144.7 %reduce-scatter.31.cloned.1.call-start = ((), (), s32[]{:S(2)}) async-start(), calls=%async_computation.29 | async-start | bytes 1966080 | tf_op jit(solution)/shard_map/reduce_scatter | solution.py:120
  578.5 70.8 %reduce-scatter.29.cloned.1.call-start = ((), (), s32[]{:S(2)}) async-start(), calls=%async_computation.27 | async-start | bytes 1966080 | tf_op jit(solution)/shard_map/reduce_scatter | solution.py:111
  585.8 104.8 %all-gather.33.cloned.1.call-start = ((), (), s32[]{:S(2)}) async-start(), calls=%async_computation.30 | async-start | bytes 1966080 | tf_op jit(solution)/shard_map/all_gather | solution.py:107
  654.5 202.0 %reduce-scatter.33.cloned.1.call-start = ((), (), s32[]{:S(2)}) async-start(), calls=%async_computation.31 | async-start | bytes 1966080 | tf_op jit(solution)/shard_map/reduce_scatter | solution.py:120
  734.6 36.0 %collective-permute-start.2 = (bf16[2,16,128,192]{2,3,1,0:T(8,128)(2,1)}, bf16[2,16,128,192]{2,3,1,0:T(8,128)(2,1)}, u32[]{:S(2)}, u32[]{:S(2)}) collective-permute-start(bf16[2,16,128,192]{2,3,1,0:T(8,128)(2,1)} %copy.314), channel_id=1, source_target_pairs={{0,8},{4,12},{8,0},{12,4},{16,24},{20,28},{24,16},{28,20},{1,9},{5... | collective-permute-start | bytes 4718600 | tf_op jit(solution)/shard_map/ppermute | solution.py:18
  782.0 14.6 %collective-permute-start.3 = (bf16[2,16,64,192]{3,2,1,0:T(8,128)(2,1)}, bf16[2,16,64,192]{3,2,1,0:T(8,128)(2,1)}, u32[]{:S(2)}, u32[]{:S(2)}) collective-permute-start(bf16[2,16,64,192]{3,2,1,0:T(8,128)(2,1)} %select_convert_fusion.1), channel_id=1, source_target_pairs={{0,4},{4,0},{8,12},{12,8},{16,20},{20,16},{24,28},{28,24},{1,5},{5... | collective-permute-start | bytes 2359304 | tf_op jit(solution)/shard_map/ppermute | solution.py:18
  821.6 80.1 %all-gather.35.cloned.1.call-start = ((), (), s32[]{:S(2)}) async-start(), calls=%async_computation.32 | async-start | bytes 1966080 | tf_op jit(solution)/shard_map/all_gather | solution.py:107
  865.7 80.6 %reduce-scatter.35.cloned.1.call-start = ((), (), s32[]{:S(2)}) async-start(), calls=%async_computation.33 | async-start | bytes 1966080 | tf_op jit(solution)/shard_map/reduce_scatter | solution.py:120
  912.1 79.5 %all-gather.37.cloned.1.call-start = ((), (), s32[]{:S(2)}) async-start(), calls=%async_computation.34 | async-start | bytes 1966080 | tf_op jit(solution)/shard_map/all_gather | solution.py:107
  955.6 91.2 %reduce-scatter.53.cloned.1.call-start = ((), (), s32[]{:S(2)}) async-start(), calls=%async_computation.43 | async-start | bytes 884736
  959.6 115.4 %reduce-scatter.51.cloned.1.call-start = ((), (), s32[]{:S(2)}) async-start(), calls=%async_computation.42 | async-start | bytes 884736
  1012.3 92.2 %reduce-scatter.37.cloned.1.call-start = ((), (), s32[]{:S(2)}) async-start(), calls=%async_computation.35 | async-start | bytes 1966080 | tf_op jit(solution)/shard_map/reduce_scatter | solution.py:120
  1018.5 138.1 %reduce-scatter.49.cloned.1.call-start = ((), (), s32[]{:S(2)}) async-start(), calls=%async_computation.41 | async-start | bytes 2654208 | tf_op jit(solution)/shard_map/reduce_scatter | solution.py:359
  1022.9 173.6 %reduce-scatter.47.cloned.1.call-start = ((), (), s32[]{:S(2)}) async-start(), calls=%async_computation.40 | async-start | bytes 2654208 | tf_op jit(solution)/shard_map/reduce_scatter | solution.py:357
  1028.0 214.8 %reduce-scatter.45.cloned.1.call-start = ((), (), s32[]{:S(2)}) async-start(), calls=%async_computation.39 | async-start | bytes 2654208 | tf_op jit(solution)/shard_map/reduce_scatter | solution.py:354
  1031.2 258.2 %reduce-scatter.43.cloned.1.call-start = ((), (), s32[]{:S(2)}) async-start(), calls=%async_computation.38 | async-start | bytes 2654208 | tf_op jit(solution)/shard_map/reduce_scatter | solution.py:359
  1036.2 299.5 %reduce-scatter.41.cloned.1.call-start = ((), (), s32[]{:S(2)}) async-start(), calls=%async_computation.37 | async-start | bytes 2654208 | tf_op jit(solution)/shard_map/reduce_scatter | solution.py:357
  1040.6 341.7 %reduce-scatter.39.cloned.1.call-start = ((), (), s32[]{:S(2)}) async-start(), calls=%async_computation.36 | async-start | bytes 2654208 | tf_op jit(solution)/shard_map/reduce_scatter | solution.py:354
  1045.1 62.2 %copy-start.56 = (f32[768]{0:T(1024)S(1)}, f32[768]{0:T(1024)}, u32[]{:S(2)}) copy-start(f32[768]{0:T(1024)} %get-tuple-element.34) | copy-start | bytes 9220
  1045.1 62.2 %copy-start.57 = (f32[768]{0:T(1024)S(1)}, f32[768]{0:T(1024)}, u32[]{:S(2)}) copy-start(f32[768]{0:T(1024)} %get-tuple-element.26) | copy-start | bytes 9220
  1045.1 62.2 %copy-start.58 = (f32[768]{0:T(1024)S(1)}, f32[768]{0:T(1024)}, u32[]{:S(2)}) copy-start(f32[768]{0:T(1024)} %get-tuple-element.77) | copy-start | bytes 9220
  1045.1 62.2 %copy-start.59 = (f32[768]{0:T(1024)S(1)}, f32[768]{0:T(1024)}, u32[]{:S(2)}) copy-start(f32[768]{0:T(1024)} %get-tuple-element.101) | copy-start | bytes 9220
  1045.1 62.2 %copy-start.60 = (f32[768]{0:T(1024)S(1)}, f32[768]{0:T(1024)}, u32[]{:S(2)}) copy-start(f32[768]{0:T(1024)} %get-tuple-element.36) | copy-start | bytes 9220
  1045.1 62.2 %copy-start.61 = (f32[768]{0:T(1024)S(1)}, f32[768]{0:T(1024)}, u32[]{:S(2)}) copy-start(f32[768]{0:T(1024)} %get-tuple-element.28) | copy-start | bytes 9220
  1045.1 62.2 %copy-start.62 = (f32[768]{0:T(1024)S(1)}, f32[768]{0:T(1024)}, u32[]{:S(2)}) copy-start(f32[768]{0:T(1024)} %get-tuple-element.79) | copy-start | bytes 9220
  1045.1 62.2 %copy-start.63 = (f32[768]{0:T(1024)S(1)}, f32[768]{0:T(1024)}, u32[]{:S(2)}) copy-start(f32[768]{0:T(1024)} %get-tuple-element.38) | copy-start | bytes 9220
  1045.1 62.2 %copy-start.64 = (f32[768]{0:T(1024)S(1)}, f32[768]{0:T(1024)}, u32[]{:S(2)}) copy-start(f32[768]{0:T(1024)} %get-tuple-element.30) | copy-start | bytes 9220
  1045.2 62.2 %copy-start.65 = (f32[768]{0:T(1024)S(1)}, f32[768]{0:T(1024)}, u32[]{:S(2)}) copy-start(f32[768]{0:T(1024)} %get-tuple-element.81) | copy-start | bytes 9220
  1045.2 109.3 %copy-start.15 = (f32[256,768]{1,0:T(8,128)S(1)}, f32[256,768]{1,0:T(8,128)}, u32[]{:S(2)}) copy-start(f32[256,768]{1,0:T(8,128)} %copy-done.14) | copy-start | bytes 2359300
  (70 other events, 780.9 us)
Sparse Core Ops, SparseCore 0:
  66.2 37.2 all-gather.14
  117.9 34.3 reduce-scatter.22
  221.3 35.2 reduce-scatter.24
  425.2 33.2 reduce-scatter.26
  578.6 34.1 reduce-scatter.30
  615.0 34.2 reduce-scatter.28
  821.8 34.7 reduce-scatter.32
  912.2 34.1 reduce-scatter.34
Sparse Core Ops, SparseCore 1:
  120.7 22.9 all-gather.18
  155.7 35.9 all-gather.16
  194.0 22.7 all-gather.20
  261.2 35.9 all-gather.22
  428.4 21.8 all-gather.26
  463.1 35.9 all-gather.24
  501.4 22.7 all-gather.28
  525.6 36.9 all-gather.30
  654.6 35.9 all-gather.32
  865.8 35.9 all-gather.34
  955.6 35.9 all-gather.36
  994.8 33.8 reduce-scatter.52
  1031.6 35.0 reduce-scatter.50
  1069.0 35.3 reduce-scatter.36
  1108.4 41.6 reduce-scatter.48
  1154.3 42.1 reduce-scatter.46
  1200.5 42.3 reduce-scatter.44
  1247.1 42.3 reduce-scatter.42
  1293.3 42.3 reduce-scatter.40
  1340.0 42.3 reduce-scatter.38
where the time goes:
time: 1400 us; the launch traced here: 1390 us
  waiting for transfers between devices  747 us (53%)
  blocking collectives  211 us (15%)
  local copies, waits for them, and re-layouts  173 us (12%)
  matrix products  125 us (9%)
  other arithmetic  109 us (8%)
  between operations  19.7 us (1%)
    all_gather x4, waiting for transfers between devices, share_grads(): return lax.all_gather(values, 'mp', axis=0, tiled=True)  140 us
    reduce_scatter x4, waiting for transfers between devices, reduce_rows(): lax.psum_scatter(jnp.dot(values, weight, preferred_element_type=jnp.float...  124 us
    reduce_scatter x4, waiting for transfers between devices, back_rows(): lax.psum_scatter(apply(jnp.int32(0), lax.axis_size('mp') * rows).astype(j...  123 us
    unnamed x4, blocking collectives  121 us
    reduce_scatter x2, waiting for transfers between devices, settle(): lax.psum_scatter(large[0], 'dp', scatter_dimension=0, tiled=True)  93 us
    reduce_scatter x2, waiting for transfers between devices, settle(): lax.psum_scatter(large[3], 'dp', scatter_dimension=0, tiled=True)  86.1 us
    all_gather x4, waiting for transfers between devices, share_rows(): return lax.all_gather(values, 'mp', axis=0, tiled=True)  61.7 us
    all_gather x2, blocking collectives, fetch(): lax.all_gather(outweight.astype(half), 'dp', axis=1, tiled=True)  47.8 us
  transfers between devices with their start and end apart: 32, of which 24 were waited for; matrix products, arithmetic and copies ran while one was open for 12% of the time, Pallas kernels for 0%

commit v1 on v0

v1 whole, which is shorter than its diff:
```python
import functools

import jax
import jax.numpy as jnp
import numpy as np
from jax import lax
from jax.experimental import pallas as pl
from jax.experimental.pallas import tpu as pltpu
from jax.sharding import PartitionSpec as P

MESH = pl.DeviceIdType.MESH
HEAD = 64
SIDE = 16
TUBE = 4
FRAME = SIDE * SIDE
CLIP = 4096
EPS = 1e-06
INNER = 8
F32 = jnp.float32
BF16 = jnp.bfloat16


def mm(left, right):
    return lax.dot_general(left, right, (((1,), (0,)), ((), ())), preferred_element_type=F32)


def mm_t(left, right):
    return lax.dot_general(left, right, (((1,), (1,)), ((), ())), preferred_element_type=F32)


def t_mm(left, right):
    return lax.dot_general(left, right, (((0,), (0,)), ((), ())), preferred_element_type=F32)


def exact(left, right, dims):
    return lax.dot_general(
        left, right, (dims, ((), ())), precision=lax.Precision.HIGHEST, preferred_element_type=F32
    )


def flip(value, weight):
    bit = (value // weight) % 2
    return value + weight * (1 - 2 * bit)


def flip_by(value, key):
    weight = 1
    while key:
        if key & 1:
            value = flip(value, weight)
        key >>= 1
        weight *= 2
    return value


def unit_rows(values):
    center = values - jnp.mean(values, axis=-1, keepdims=True)
    spread = jnp.mean(center * center, axis=-1, keepdims=True)
    scale = lax.rsqrt(spread + EPS)
    return center * scale, scale


def kernel(
    sizes,
    x_ref,
    g_ref,
    ws_ref,
    small_ref,
    swap_ref,
    tiles_ref,
    mask_ref,
    out_ref,
    ig_ref,
    wg_ref,
    sg_ref,
    W,
    SG,
    SV,
    BI,
    BU,
    H,
    M,
    NB,
    NT,
    GT,
    PK,
    CT,
    HID,
    GP,
    PR,
    ACC,
    GR,
    SGR,
    RES,
    SB,
    RB,
    HS,
    CS,
    US,
    PS,
    LS,
    AR,
    zs,
    zr,
    a1s,
    a1r,
    b1s,
    b1r,
    a2s,
    a2r,
    b2s,
    b2r,
    cs,
    cr,
    vs,
    vr,
    ts,
    tr,
    ss,
    sr,
    rs,
    rr,
    free_x,
    free_y,
    free_z,
    free_c,
    WG,
    ls,
):
    outer, nmp, d, rows = sizes
    per = INNER
    half = d // 2
    dp = lax.axis_index("dp")
    z = lax.axis_index("mp")
    low = dp % outer
    q = dp // outer
    c = q % 2
    x = (q // 2) % 2
    y = q // 4
    oc, ox, oy = 1 - c, 1 - x, 1 - y
    members = CLIP // FRAME
    dpc = members // nmp
    me = (dp % dpc) * nmp + z

    def place(cc, xx, yy):
        return (yy * 4 + xx * 2 + cc) * outer + low

    to_c = (place(oc, x, y), z)
    to_x = (place(c, ox, y), z)
    to_y = (place(c, x, oy), z)

    def to_z(zz):
        return (dp, zz)

    def to_member(f):
        return ((dp // dpc) * dpc + f // nmp, f % nmp)

    def send(src, dst, s_sem, r_sem, device):
        pltpu.make_async_remote_copy(
            src_ref=src, dst_ref=dst, send_sem=s_sem, recv_sem=r_sem, device_id=device, device_id_type=MESH
        ).start()

    def sent(src, s_sem):
        pltpu.make_async_remote_copy(
            src_ref=src, dst_ref=src, send_sem=s_sem, recv_sem=s_sem, device_id=to_c, device_id_type=MESH
        ).wait_send()

    def got(dst, r_sem):
        pltpu.make_async_remote_copy(
            src_ref=dst, dst_ref=dst, send_sem=r_sem, recv_sem=r_sem, device_id=to_c, device_id_type=MESH
        ).wait_recv()

    def keep(src, dst, n):
        return pltpu.make_async_copy(src, dst, ls.at[n])

    for m in range(6):
        keep(ws_ref.at[m], W.at[m, z, y, x, c], m).start()
    keep(x_ref, ACC, 6).start()

    barrier = pltpu.get_barrier_semaphore()
    for key in range(1, members):
        pl.semaphore_signal(barrier, inc=1, device_id=to_member(flip_by(me, key)), device_id_type=MESH)
    for device in (to_c, to_x, to_y):
        pl.semaphore_signal(barrier, inc=1, device_id=device, device_id_type=MESH)
    pl.semaphore_wait(barrier, members - 1 + 3)

    def z_start(m):
        for key in range(1, nmp):
            zz = flip_by(z, key)
            ref = W.at[m, z, y, x, c]
            send(ref, ref, zs.at[m, zz], zr.at[m, z], to_z(zz))

    def g1(m, k):
        zz = flip_by(z, k)
        if k:
            got(W.at[m, zz, y, x, c], zr.at[m, zz])
        t = m * nmp + k
        left = W.at[m, zz, y, x, c, :, pl.ds(0, half)]
        right = W.at[m, zz, y, x, c, :, pl.ds(half, half)]
        send(left, left, a1s.at[t], a1r.at[t], to_x)
        send(right, right, b1s.at[t], b1r.at[t], to_y)

    def g2(m, k):
        zz = flip_by(z, k)
        t = m * nmp + k
        got(W.at[m, zz, y, ox, c, :, pl.ds(0, half)], a1r.at[t])
        left = W.at[m, zz, y, :, c, :, pl.ds(0, half)]
        send(left, left, a2s.at[t], a2r.at[t], to_y)
        got(W.at[m, zz, oy, x, c, :, pl.ds(half, half)], b1r.at[t])
        right = W.at[m, zz, :, x, c, :, pl.ds(half, half)]
        send(right, right, b2s.at[t], b2r.at[t], to_x)

    def g3(m, k):
        zz = flip_by(z, k)
        t = m * nmp + k
        got(W.at[m, zz, oy, :, c, :, pl.ds(0, half)], a2r.at[t])
        got(W.at[m, zz, :, ox, c, :, pl.ds(half, half)], b2r.at[t])
        whole = W.at[m, zz, :, :, c]
        send(whole, whole, cs.at[t], cr.at[t], to_c)

    def g4(m, k):
        zz = flip_by(z, k)
        t = m * nmp + k
        got(W.at[m, zz, :, :, oc], cr.at[t])

    def g_done(m):
        for key in range(1, nmp):
            zz = flip_by(z, key)
            sent(W.at[m, z, y, x, c], zs.at[m, zz])
        for k in range(nmp):
            zz = flip_by(z, k)
            t = m * nmp + k
            sent(W.at[m, zz, y, x, c, :, pl.ds(0, half)], a1s.at[t])
            sent(W.at[m, zz, y, x, c, :, pl.ds(half, half)], b1s.at[t])
            sent(W.at[m, zz, y, :, c, :, pl.ds(0, half)], a2s.at[t])
            sent(W.at[m, zz, :, x, c, :, pl.ds(half, half)], b2s.at[t])
            sent(W.at[m, zz, :, :, c], cs.at[t])

    total = 6 * nmp

    def advance(t, base=0, last=total):
        def at(s):
            return base + s // nmp, s % nmp

        def ranged(s, stage):
            if isinstance(base, int) or s < 3 * nmp:
                if s < total:
                    stage(*at(s))
            else:
                pl.when(base == 0)(lambda: stage(*at(s)))

        def first(m, k):
            if k == 0:
                if isinstance(m, int):
                    if m + 1 < 6:
                        z_start(m + 1)
                else:
                    pl.when(m + 1 < 6)(lambda: z_start(m + 1))
            g1(m, k)

        ranged(t, first)
        if t >= 1:
            ranged(t - 1, g2)
        if t >= 2:
            ranged(t - 2, g3)
        if t >= 3:
            ranged(t - 3, g4)

    def release(m):
        g_done(m)
        pl.semaphore_signal(free_x.at[m], inc=1, device_id=to_x, device_id_type=MESH)
        pl.semaphore_signal(free_y.at[m], inc=1, device_id=to_y, device_id_type=MESH)
        for key in range(1, nmp):
            pl.semaphore_signal(free_z.at[m, z], inc=1, device_id=to_z(flip_by(z, key)), device_id_type=MESH)

    def may_send(m):
        pl.semaphore_wait(free_x.at[m], 1)
        pl.semaphore_wait(free_y.at[m], 1)

    def r1(m, k):
        t = m * nmp + k
        send(
            W.at[m, k, :, ox, c, :, pl.ds(0, half)],
            W.at[m, k, :, ox, oc, :, pl.ds(0, half)],
            a1s.at[t],
            a1r.at[t],
            to_x,
        )
        send(
            W.at[m, k, oy, :, c, :, pl.ds(half, half)],
            W.at[m, k, oy, :, oc, :, pl.ds(half, half)],
            b1s.at[t],
            b1r.at[t],
            to_y,
        )

    def add_to(dst, src):
        dst[...] = (dst[...].astype(F32) + src[...].astype(F32)).astype(BF16)

    def r2(m, k):
        t = m * nmp + k
        src = W.at[m, k, :, x, oc, :, pl.ds(0, half)]
        got(src, a1r.at[t])
        add_to(W.at[m, k, :, x, c, :, pl.ds(0, half)], src)
        send(
            W.at[m, k, oy, x, c, :, pl.ds(0, half)],
            W.at[m, k, oy, ox, oc, :, pl.ds(0, half)],
            a2s.at[t],
            a2r.at[t],
            to_y,
        )
        src = W.at[m, k, y, :, oc, :, pl.ds(half, half)]
        got(src, b1r.at[t])
        add_to(W.at[m, k, y, :, c, :, pl.ds(half, half)], src)
        send(
            W.at[m, k, y, ox, c, :, pl.ds(half, half)],
            W.at[m, k, oy, ox, oc, :, pl.ds(half, half)],
            b2s.at[t],
            b2r.at[t],
            to_x,
        )

    def r3(m, k):
        t = m * nmp + k
        src = W.at[m, k, y, ox, oc, :, pl.ds(0, half)]
        got(src, a2r.at[t])
        add_to(W.at[m, k, y, x, c, :, pl.ds(0, half)], src)
        src = W.at[m, k, oy, x, oc, :, pl.ds(half, half)]
        got(src, b2r.at[t])
        add_to(W.at[m, k, y, x, c, :, pl.ds(half, half)], src)

        @pl.when(k != z)
        def _():
            pl.semaphore_wait(free_z.at[m, k], 1)
            send(W.at[m, k, y, x, c], W.at[m, z, oy, ox, oc], zs.at[m, k], zr.at[m, z], to_z(k))

    def r4(m):
        sum_ = W[m, z, y, x, c].astype(F32)
        for key in range(1, nmp):
            zz = flip_by(z, key)
            src = W.at[m, zz, oy, ox, oc]
            got(src, zr.at[m, zz])
            sum_ = sum_ + src[...].astype(F32)
        if m < 3:
            keep(WG.at[m], wg_ref.at[m + 3], m + 3).wait()
        WG[m % 3] = sum_
        keep(WG.at[m % 3], wg_ref.at[m], m).start()

    def r_done(m):
        for key in range(1, nmp):
            zz = flip_by(z, key)
            sent(W.at[m, zz, y, x, c], zs.at[m, zz])
        for k in range(nmp):
            t = m * nmp + k
            sent(W.at[m, k, :, ox, c, :, pl.ds(0, half)], a1s.at[t])
            sent(W.at[m, k, oy, :, c, :, pl.ds(half, half)], b1s.at[t])
            sent(W.at[m, k, oy, x, c, :, pl.ds(0, half)], a2s.at[t])
            sent(W.at[m, k, y, ox, c, :, pl.ds(half, half)], b2s.at[t])

    def each(stage):
        def step(k, _):
            stage(k)
            return 0
        lax.fori_loop(0, nmp, step, 0)

    def swap_start(i):
        RB[i, pl.ds(me, 1)] = SB[i, pl.ds(me, 1)]
        for key in range(1, members):
            f = flip_by(me, key)
            send(SB.at[i, f], RB.at[i, me], ts.at[i, key], tr.at[i, key], to_member(f))

    def swap_wait(i):
        for key in range(1, members):
            got(RB.at[i, flip_by(me, key)], tr.at[i, key])

    def swap_done(i):
        for key in range(1, members):
            sent(SB.at[i, flip_by(me, key)], ts.at[i, key])

    def rows_of(ref, i):
        return ref[i].reshape(rows, d)

    for m in range(6):
        keep(ws_ref.at[m], W.at[m, z, y, x, c], m).wait()
    z_start(0)
    SG[z, y, x, c] = small_ref[...]
    for key in range(1, nmp):
        zz = flip_by(z, key)
        ref = SG.at[z, y, x, c]
        send(ref, ref, vs.at[zz], vr.at[z], to_z(zz))
    advance(0)
    swap = swap_ref[...]
    SB[0] = mm(swap, g_ref[...]).astype(BF16).reshape(members, rows // members, d)
    swap_start(0)
    keep(x_ref, ACC, 6).wait()
    H[0] = exact(swap.astype(F32), ACC[...], ((1,), (0,)))
    for key in range(1, nmp):
        zz = flip_by(z, key)
        got(SG.at[zz, y, x, c], vr.at[zz])
    ref = SG.at[:, y, x, c]
    send(ref, ref, vs.at[nmp], vr.at[nmp], to_x)
    advance(1)
    got(SG.at[:, y, ox, c], vr.at[nmp])
    ref = SG.at[:, y, :, c]
    send(ref, ref, vs.at[nmp + 1], vr.at[nmp + 1], to_y)
    advance(2)
    got(SG.at[:, oy, :, c], vr.at[nmp + 1])
    ref = SG.at[:, :, :, c]
    send(ref, ref, vs.at[nmp + 2], vr.at[nmp + 2], to_c)
    advance(3)
    got(SG.at[:, :, :, oc], vr.at[nmp + 2])

    lane = lax.broadcasted_iota(jnp.int32, (1, d), 1)
    third = d // nmp
    tall = SG[...].reshape(nmp * per * 16, 128)
    spread = mm(tall, tiles_ref[0]).reshape(nmp * per, 16, d)
    spread = jnp.sum(spread * mask_ref[0:nmp * per].reshape(nmp * per, 1, d), axis=0)
    SV[0, 0:6] = spread[0:6]
    SV[1, 0:6] = spread[6:12]
    is_q = (lane < third).astype(F32)
    is_v = jnp.logical_and(lane >= third, lane < 2 * third).astype(F32)
    spread_in = mm(tall, tiles_ref[1]).reshape(nmp, per, 16, d)
    spread_up = mm(tall, tiles_ref[2]).reshape(nmp, per, 16, d)
    mask_in = mask_ref[nmp * per:nmp * per + per].reshape(per, 1, d)
    mask_up = mask_ref[nmp * per + per:nmp * per + 2 * per].reshape(per, 1, d)
    for k in range(nmp):
        one = jnp.sum(spread_in[k] * mask_in, axis=0)
        two = jnp.sum(spread_up[k] * mask_up, axis=0)
        for b in range(2):
            BI[b, k] = one[12 + 2 * b:13 + 2 * b] * is_q + one[13 + 2 * b:14 + 2 * b] * is_v
            BU[b, k] = two[b:b + 1]
    advance(4)
    advance(5)
    advance(6)

    lane2 = lax.broadcasted_iota(jnp.int32, (1, 256), 1)
    heads = third // HEAD

    def head_mask(lead):
        return jnp.logical_and(lane2 >= lead * HEAD, lane2 < lead * HEAD + HEAD).astype(F32).astype(BF16)

    q_masks = [head_mask(h) for h in range(heads)]
    v_masks = [head_mask(h + 1) for h in range(heads)]
    scale = HEAD ** (-0.5)
    wide = 5 * 128

    def flat(values):
        return values.reshape(d, values.shape[-1])

    def lower(values):
        return values.reshape(half, values.shape[-1])

    def tall_view(values):
        return values.T.astype(BF16).reshape(2, 2, 2, d // per, rows)

    def forward(b, _):
        m = 3 * b
        h = H[b]
        unit, _s = unit_rows(h)
        normed = unit * SV[b, 0:1] + SV[b, 1:2]
        NB[...] = normed.astype(BF16)
        NT[b, 0] = tall_view(normed)
        ACC[...] = h + SV[b, 2:3]

        def attend(k, _):
            packed = (mm(NB[...], flat(W[m, k, :, :, :, :, 0:wide])) + BI[b, k, :, 0:wide]).astype(BF16)
            PK[b, k] = packed
            qs = packed[:, 0:256] * BF16(scale)
            vv = packed[:, 128:384]
            kk = packed[:, 384:640]
            mixed = jnp.zeros((rows, 256), F32)
            for h in range(heads):
                scores = mm_t(qs * q_masks[h], kk)
                expo = jnp.exp(scores - jnp.max(scores, axis=-1, keepdims=True))
                probs = (expo * (1.0 / jnp.sum(expo, axis=-1, keepdims=True))).astype(BF16)
                PR[b, k, h] = probs
                mixed += mm(probs, vv * v_masks[h])
            mixed = mixed.astype(BF16)
            CT[b, k] = mixed
            ACC[...] += mm_t(mixed, flat(W[m, k, :, :, :, :, d - 256:d]))
            return 0

        lax.fori_loop(0, nmp, attend, 0)
        for t in range(7, 11):
            advance(t, m)
        middle = ACC[...]
        M[b] = middle
        unit, _s = unit_rows(middle)
        normed = unit * SV[b, 3:4] + SV[b, 4:5]
        NB[...] = normed.astype(BF16)
        NT[b, 1] = tall_view(normed)
        ACC[...] = middle + SV[b, 5:6]

        def expand(k, _):
            upper = mm(NB[...], flat(W[m + 1, k])) + BU[b, k]
            cdf = 0.5 + 0.5 * lax.erf(upper * (0.5 ** 0.5))
            HID[b, k] = (upper * cdf).astype(BF16)
            density = jnp.exp(-0.5 * upper * upper) * ((2 * np.pi) ** -0.5)
            GP[b, k] = (cdf + upper * density).astype(BF16)
            return 0

        lax.fori_loop(0, nmp, expand, 0)
        for t in range(11, 15):
            advance(t, m)

        def contract(k, _):
            ACC[...] += mm_t(HID[b, k], flat(W[m + 2, k]))
            return 0

        lax.fori_loop(0, nmp, contract, 0)
        SB[1 + b] = ACC[...].astype(BF16).reshape(members, rows // members, d)
        swap_start(1 + b)
        for t in range(15, 19):
            advance(t, m)

        @pl.when(b == 0)
        def _():
            swap_wait(1)
            H[1] = rows_of(RB, 1).astype(F32)
        return 0

    lax.fori_loop(0, 2, forward, 0)

    swap_wait(0)
    GR[...] = rows_of(RB, 0).astype(F32)

    def norm_back(grad, start, gain):
        unit, scale = unit_rows(start)
        lifted = grad * gain
        back = scale * (
            lifted
            - jnp.mean(lifted, axis=-1, keepdims=True)
            - unit * jnp.mean(lifted * unit, axis=-1, keepdims=True)
        )
        return back, jnp.sum(grad * unit, axis=0, keepdims=True), jnp.sum(grad, axis=0, keepdims=True)

    def to_sibling(src, dst, n):
        send(src, dst, ss.at[n], sr.at[n], to_c)

    def backward(step, _):
        b = 1 - step
        m = 3 * b
        row = 16 * b

        @pl.when(step == 1)
        def _():
            pl.semaphore_wait(free_c, 1)

        to_sibling(HID.at[b], HS, 0)
        to_sibling(NT.at[b, 0, :, :, oc], LS.at[0], 1)
        to_sibling(NT.at[b, 1, :, :, oc], LS.at[1], 2)
        to_sibling(CT.at[b], CS, 3)
        grad = GR[...]
        SGR[pl.ds(row + 5, 1)] = jnp.sum(grad, axis=0, keepdims=True)
        NB[...] = grad.astype(BF16)
        GT[0] = tall_view(grad)
        to_sibling(GT.at[0, :, :, oc], LS.at[2], 4)

        def shrink(k, _):
            hidden_grad = mm(NB[...], flat(W[m + 2, k]))
            upper_grad = (GP[b, k].astype(F32) * hidden_grad).astype(BF16)
            GP[b, k] = upper_grad
            to_sibling(GP.at[b, k], US.at[k], 6 + k)
            SGR[pl.ds(row + 10 + k, 1)] = jnp.sum(upper_grad.astype(F32), axis=0, keepdims=True)
            return 0

        lax.fori_loop(0, nmp, shrink, 0)
        release(m + 2)
        got(HS, sr.at[0])
        got(LS.at[2], sr.at[4])
        may_send(m + 2)

        def down_grad(k, _):
            own = mm(lower(GT[0, :, :, c]), HID[b, k]) + mm(lower(LS[2]), HS[k])
            W[m + 2, k, :, :, c] = own.astype(BF16).reshape(2, 2, d // per, d)
            r1(m + 2, k)
            return 0

        lax.fori_loop(0, nmp, down_grad, 0)
        ACC[...] = jnp.zeros_like(ACC)

        def spread_up(k, _):
            ACC[...] += mm_t(GP[b, k], flat(W[m + 1, k]))
            return 0

        lax.fori_loop(0, nmp, spread_up, 0)
        release(m + 1)
        for k in range(nmp):
            got(US.at[k], sr.at[6 + k])
        got(LS.at[1], sr.at[2])
        may_send(m + 1)

        @pl.when(step == 1)
        def _():
            each(functools.partial(r2, 3))
            each(functools.partial(r3, 4))
            r4(5)

        def up_grad(k, _):
            own = mm(lower(NT[b, 1, :, :, c]), GP[b, k]) + mm(lower(LS[1]), US[k])
            W[m + 1, k, :, :, c] = own.astype(BF16).reshape(2, 2, d // per, d)
            r1(m + 1, k)
            return 0

        lax.fori_loop(0, nmp, up_grad, 0)
        back, gain_grad, bias_grad = norm_back(ACC[...], M[b], SV[b, 3:4])
        SGR[pl.ds(row + 3, 1)] = gain_grad
        SGR[pl.ds(row + 4, 1)] = bias_grad
        middle_grad = GR[...] + back
        GR[...] = middle_grad
        SGR[pl.ds(row + 2, 1)] = jnp.sum(middle_grad, axis=0, keepdims=True)
        NB[...] = middle_grad.astype(BF16)
        GT[1] = tall_view(middle_grad)
        to_sibling(GT.at[1, :, :, oc], LS.at[3], 5)
        ACC[...] = jnp.zeros_like(ACC)
        each(functools.partial(r2, m + 2))

        @pl.when(step == 1)
        def _():
            each(functools.partial(r3, 3))
            r4(4)

        def attend_back(k, _):
            mixed_grad = mm(NB[...], flat(W[m, k, :, :, :, :, d - 256:d])).astype(BF16)
            packed = PK[b, k]
            qs = packed[:, 0:256] * BF16(scale)
            vv = packed[:, 128:384]
            kk = packed[:, 384:640]
            q_grad = jnp.zeros((rows, 256), F32)
            k_grad = jnp.zeros((rows, 256), F32)
            v_grad = jnp.zeros((rows, 256), F32)
            for h in range(heads):
                part = mixed_grad * v_masks[h]
                probs_low = PR[b, k, h]
                probs = probs_low.astype(F32)
                weighted = probs * mm_t(part, vv)
                score_grad = (weighted - probs * jnp.sum(weighted, axis=-1, keepdims=True)).astype(BF16)
                q_grad += mm(score_grad, kk * q_masks[h])
                k_grad += t_mm(score_grad, qs * q_masks[h])
                v_grad += t_mm(probs_low, part)
            q_grad = q_grad * scale
            packed_grad = jnp.concatenate(
                [q_grad[:, 0:128], q_grad[:, 128:256] + v_grad[:, 0:128], v_grad[:, 128:256], k_grad], axis=1
            ).astype(BF16)
            PK[b, k] = packed_grad
            to_sibling(PK.at[b, k], PS.at[k], 10 + k)
            SGR[pl.ds(row + 6 + k, 1), 0:wide] = jnp.sum(packed_grad.astype(F32), axis=0, keepdims=True)
            ACC[...] += mm_t(packed_grad, flat(W[m, k, :, :, :, :, 0:wide]))
            return 0

        lax.fori_loop(0, nmp, attend_back, 0)
        release(m)
        back, gain_grad, bias_grad = norm_back(ACC[...], H[b], SV[b, 0:1])
        SGR[pl.ds(row, 1)] = gain_grad
        SGR[pl.ds(row + 1, 1)] = bias_grad
        GR[...] = GR[...] + back

        @pl.when(step == 0)
        def _():
            SB[3] = GR[...].astype(BF16).reshape(members, rows // members, d)
            swap_start(3)

        for k in range(nmp):
            got(PS.at[k], sr.at[10 + k])
        got(LS.at[0], sr.at[1])
        got(LS.at[3], sr.at[5])
        got(CS, sr.at[3])
        may_send(m)

        def in_grad(k, _):
            one = mm(lower(NT[b, 0, :, :, c]), PK[b, k]) + mm(lower(LS[0]), PS[k])
            two = mm(lower(GT[1, :, :, c]), CT[b, k]) + mm(lower(LS[3]), CS[k])
            own = jnp.concatenate(
                [one[:, 0:512], one[:, 512:640] + two[:, 0:128], two[:, 128:256]], axis=1
            ).astype(BF16)
            W[m, k, :, :, c] = own.reshape(2, 2, d // per, d)
            r1(m, k)
            return 0

        lax.fori_loop(0, nmp, in_grad, 0)

        sent(HID.at[b], ss.at[0])
        sent(NT.at[b, 0, :, :, oc], ss.at[1])
        sent(NT.at[b, 1, :, :, oc], ss.at[2])
        sent(CT.at[b], ss.at[3])
        sent(GT.at[0, :, :, oc], ss.at[4])
        sent(GT.at[1, :, :, oc], ss.at[5])
        for k in range(nmp):
            sent(GP.at[b, k], ss.at[6 + k])
            sent(PK.at[b, k], ss.at[10 + k])

        @pl.when(step == 0)
        def _():
            pl.semaphore_signal(free_c, inc=1, device_id=to_c, device_id_type=MESH)

        each(functools.partial(r2, m + 1))
        each(functools.partial(r3, m + 2))

        @pl.when(step == 1)
        def _():
            r4(3)

        @pl.when(step == 0)
        def _():
            swap_wait(3)
            GR[...] = rows_of(RB, 3).astype(F32)
        return 0

    lax.fori_loop(0, 2, backward, 0)

    peers = [to_c, to_x, to_y]
    key = 1
    while key < nmp:
        peers.append(to_z(flip_by(z, key)))
        key *= 2
    for i, device in enumerate(peers):
        send(SGR, AR.at[i], rs.at[i], rr.at[i], device)
        if i == 0:
            each(functools.partial(r2, 0))
        if i == 1:
            each(functools.partial(r3, 1))
        if i == 2:
            r4(2)
        if i == 3:
            swap_wait(2)
            M[0] = mm(swap, rows_of(RB, 2))
            keep(M.at[0], out_ref, 6).start()
            ACC[...] = exact(swap.astype(F32), GR[...], ((1,), (0,)))
            keep(ACC, ig_ref, 7).start()
        sent(SGR, rs.at[i])
        got(AR.at[i], rr.at[i])
        SGR[...] += AR[i]
    each(functools.partial(r3, 0))
    grads = SGR[...]
    own = mask_ref[pl.ds(z * per + q, 1)]
    own_in = mask_ref[pl.ds(nmp * per + q, 1)]
    own_up = mask_ref[pl.ds(nmp * per + per + q, 1)]
    turned = ((1,), (1,))
    RES[0] = exact(grads * own, tiles_ref[0].astype(F32), turned)
    RES[1] = exact(grads * own_in * is_q, tiles_ref[1].astype(F32), turned)
    RES[2] = exact(grads * own_in * is_v, tiles_ref[1].astype(F32), turned)
    RES[3] = exact(grads * own_up, tiles_ref[2].astype(F32), turned)
    sg_ref[...] = jnp.zeros_like(sg_ref)
    for b in range(2):
        sg_ref[b, 0:6] = RES[0, 16 * b:16 * b + 6]
        sg_ref[b, 6:7] = RES[1, pl.ds(16 * b + 6 + z, 1)]
        sg_ref[b, 7:8] = RES[2, pl.ds(16 * b + 6 + z, 1)]
        sg_ref[b, 8:9] = RES[3, pl.ds(16 * b + 10 + z, 1)]
    r4(1)
    r4(0)
    for m in range(3):
        keep(WG.at[m], wg_ref.at[m], m).wait()
    keep(M.at[0], out_ref, 6).wait()
    keep(ACC, ig_ref, 7).wait()
    for m in range(6):
        r_done(m)
    for i in range(4):
        swap_done(i)
    for key in range(1, nmp):
        sent(SG.at[z, y, x, c], vs.at[flip_by(z, key)])
    sent(SG.at[:, y, x, c], vs.at[nmp])
    sent(SG.at[:, y, :, c], vs.at[nmp + 1])
    sent(SG.at[:, :, :, c], vs.at[nmp + 2])


def tables(outer, ndp, nmp, d):
    n = d // (ndp * nmp)
    tiles = np.zeros((3, 128, d), np.float32)
    masks = np.zeros((nmp * INNER + 2 * INNER, d), np.float32)
    for at in range(d):
        i = at % n
        zz = (at // n) % nmp
        pp = at // (n * nmp)
        qq, lo = pp // outer, pp % outer
        tiles[0, lo * n + i, at] = 1
        masks[zz * INNER + qq, at] = 1
    third = d // nmp
    step = third // INNER
    for at in range(2 * third):
        tiles[1, at % step, at] = 1
        masks[nmp * INNER + (at % third) // step, at] = 1
    step = d // INNER
    for at in range(d):
        tiles[2, 32 + at % step, at] = 1
        masks[nmp * INNER + INNER + at // step, at] = 1
    return tiles, masks


def turn_table():
    swap = np.zeros((FRAME, FRAME), np.float32)
    across = SIDE // TUBE
    for wr in range(across):
        for i in range(TUBE):
            for wc in range(across):
                for j in range(TUBE):
                    natural = ((wr * TUBE + i) * across + wc) * TUBE + j
                    turned = ((wr * across + wc) * TUBE + i) * TUBE + j
                    swap[turned, natural] = 1
    return swap


def fused(sizes, x, grad, shards, small, ndp):
    outer, nmp, d, rows = sizes
    tiles, masks = tables(outer, ndp, nmp, d)
    members = CLIP // FRAME
    vmem = pltpu.VMEM
    dma = pltpu.SemaphoreType.DMA
    regular = pltpu.SemaphoreType.REGULAR
    block = d // INNER
    steps = 6 * nmp
    scratch = [
        vmem((6, nmp, 2, 2, 2, block, d), BF16),
        vmem((nmp, 2, 2, 2, 16, 128), BF16),
        vmem((2, 8, d), F32),
        vmem((2, nmp, 1, d), F32),
        vmem((2, nmp, 1, d), F32),
        vmem((2, rows, d), F32),
        vmem((2, rows, d), F32),
        vmem((rows, d), BF16),
        vmem((2, 2, 2, 2, 2, block, rows), BF16),
        vmem((2, 2, 2, 2, block, rows), BF16),
        vmem((2, nmp, rows, 640), BF16),
        vmem((2, nmp, rows, 256), BF16),
        vmem((2, nmp, rows, d), BF16),
        vmem((2, nmp, rows, d), BF16),
        vmem((2, nmp, d // nmp // HEAD, rows, rows), BF16),
        vmem((rows, d), F32),
        vmem((rows, d), F32),
        vmem((32, d), F32),
        vmem((4, 32, 128), F32),
        vmem((4, members, rows // members, d), BF16),
        vmem((4, members, rows // members, d), BF16),
        vmem((nmp, rows, d), BF16),
        vmem((nmp, rows, 256), BF16),
        vmem((nmp, rows, d), BF16),
        vmem((nmp, rows, 640), BF16),
        vmem((4, 2, 2, block, rows), BF16),
        vmem((3 + nmp.bit_length() - 1, 32, d), F32),
        dma((6, nmp)),
        dma((6, nmp)),
    ]
    scratch += [dma((steps,)) for _ in range(10)]
    scratch += [
        dma((nmp + 3,)),
        dma((nmp + 3,)),
        dma((4, members)),
        dma((4, members)),
        dma((14,)),
        dma((14,)),
        dma((3 + nmp.bit_length() - 1,)),
        dma((3 + nmp.bit_length() - 1,)),
        regular((6,)),
        regular((6,)),
        regular((6, nmp)),
        regular,
        vmem((3, block, d), F32),
        dma((8,)),
    ]
    return pl.pallas_call(
        functools.partial(kernel, sizes),
        out_shape=(
            jax.ShapeDtypeStruct((rows, d), F32),
            jax.ShapeDtypeStruct((rows, d), F32),
            jax.ShapeDtypeStruct((6, block, d), F32),
            jax.ShapeDtypeStruct((2, 16, 128), F32),
        ),
        in_specs=[pl.BlockSpec(memory_space=s) for s in (pl.ANY, vmem, pl.ANY, vmem, vmem, vmem, vmem)],
        out_specs=tuple(pl.BlockSpec(memory_space=s) for s in (pl.ANY, pl.ANY, pl.ANY, vmem)),
        scratch_shapes=scratch,
        compiler_params=pltpu.CompilerParams(
            collective_id=0, has_side_effects=True, vmem_limit_bytes=64 << 20
        ),
        name="two_blocks",
    )(
        x,
        grad,
        shards,
        small,
        jnp.asarray(turn_table(), BF16),
        jnp.asarray(tiles, BF16),
        jnp.asarray(masks, F32),
    )


def pack_weights(params):
    inweight, outweight, upweight, downweight = params[2], params[4], params[8], params[10]
    attention = jnp.concatenate([inweight[:, 0], inweight[:, 2], inweight[:, 1], outweight.T], axis=1)
    return [attention.astype(BF16), upweight.astype(BF16), downweight.T.astype(BF16)]


def shards_of(ndp, nmp, inputs, cotangent, mask_bits, *params):
    frame, tube = params[:12], params[12:]
    d = inputs.shape[1]
    rows = inputs.shape[0]
    outer = ndp // INNER
    groups = [[qq * outer + lo for lo in range(outer)] for qq in range(INNER)]
    weights = jnp.stack(pack_weights(frame) + pack_weights(tube))
    vectors = []
    for block in (frame, tube):
        vectors += [block[0], block[1], block[5], block[6], block[7], block[11]]
    for block in (frame, tube):
        vectors += [block[3][0], block[3][1]]
    vectors = jnp.stack(vectors).astype(BF16)
    ups = jnp.stack([frame[9], tube[9]]).astype(BF16)
    if outer > 1:
        weights = lax.all_gather(weights, "dp", axis=1, tiled=True, axis_index_groups=groups)
        vectors = lax.all_gather(vectors, "dp", axis=1, tiled=True, axis_index_groups=groups)
        ups = lax.all_gather(ups, "dp", axis=1, tiled=True, axis_index_groups=groups)
    wide = vectors.shape[1]
    small = jnp.concatenate(
        [jnp.pad(vectors, ((0, 0), (0, 32 - wide))), jnp.pad(ups, ((0, 14), (0, 0)))], axis=1
    )
    grad = (cotangent * mask_bits.astype(F32)[:, None]).astype(BF16)
    out, input_grad, wg, sg = fused((outer, nmp, d, rows), inputs, grad, weights, small, ndp)
    if outer > 1:
        wg = lax.psum_scatter(wg, "dp", scatter_dimension=1, tiled=True, axis_index_groups=groups)
        sg = lax.psum(sg, "dp", axis_index_groups=groups)
    low = lax.axis_index("dp") % outer

    def piece(values, start, size):
        size = size // outer
        if outer == 1:
            return values[start:start + size]
        return lax.dynamic_slice_in_dim(values, start + low * size, size)

    n = wide
    third = d // nmp
    results = []
    for b in range(2):
        attention, up, down = wg[3 * b], wg[3 * b + 1], wg[3 * b + 2]
        rows_ = sg[b]
        results += [
            piece(rows_[0], 0, n),
            piece(rows_[1], 0, n),
            jnp.stack([attention[:, 0:third], attention[:, 2 * third:3 * third], attention[:, third:2 * third]], axis=1),
            jnp.stack([piece(rows_[6], 0, n), piece(rows_[7], 0, n)]),
            attention[:, 3 * third:].T,
            piece(rows_[2], 0, n),
            piece(rows_[3], 0, n),
            piece(rows_[4], 0, n),
            up,
            piece(rows_[8], 32, 4 * n),
            down.T,
            piece(rows_[5], 0, n),
        ]
    return (out, input_grad) + tuple(results)


def solution(mesh):
    rows = P(("dp", "mp"), None)
    small = P(("dp", "mp"))
    block = (
        small,
        small,
        P("dp", None, "mp"),
        P(None, ("mp", "dp")),
        P("mp", "dp"),
        small,
        small,
        small,
        P("dp", "mp"),
        P(("mp", "dp")),
        P("mp", "dp"),
        small,
    )
    return jax.shard_map(
        functools.partial(shards_of, mesh.shape["dp"], mesh.shape["mp"]),
        mesh=mesh,
        in_specs=(rows, rows, small) + block + block,
        out_specs=(rows, rows) + block + block,
        check_vma=False,
    )
```

time: 1400 us -> 340 us (0.24)
  waiting for transfers between devices: 747 us -> 0 us
  Pallas kernels: 0 us -> 311 us
  blocking collectives: 211 us -> 0 us
  local copies, waits for them, and re-layouts: 173 us -> 10.8 us
  matrix products: 125 us -> 0 us
  other arithmetic: 109 us -> 17.2 us
  between operations: 19.7 us -> 0.8 us
    reduce_scatter x14 -> x0, waiting for transfers between devices: 473 us -> none  [the longest x4 124 us: reduce_rows(): lax.psum_scatter(jnp.dot(values, weight, preferred_element_type=jnp.float...]
    pallas_call x0 -> x1, Pallas kernels: none -> 311 us  [fused(): pl.pallas_call(functools.partial(kernel, sizes), out_shape=(jax.ShapeDtyp...]
    all_gather x12 -> x0, waiting for transfers between devices: 236 us -> none  [the longest x4 140 us: share_grads(): return lax.all_gather(values, 'mp', axis=0, tiled=True)]
    unnamed x4 -> x0, blocking collectives: 121 us -> none
    dot_general x34 -> x0, matrix products: 119 us -> none  [the longest x6 29.7 us: against(): lax.dot_general(left, weight, (((1,), (1,)), ((), ())), preferred_element...]
    all_gather x6 -> x0, blocking collectives: 89.7 us -> none  [the longest x2 47.8 us: fetch(): lax.all_gather(outweight.astype(half), 'dp', axis=1, tiled=True)]
    another operation x30 -> x1, local copies, waits for them, and re-layouts: 60.9 us -> 0.06 us  [shards_of(): vectors = jnp.stack(vectors).astype(BF16)]
    convert_element_type x49 -> x2, other arithmetic: 50 us -> 1.54 us  [shards_of(): grad = (cotangent * mask_bits.astype(F32)[:, None]).astype(BF16)]
  transfers between devices with their start and end apart: 32 -> 0, of which waited for: 24 -> 0; matrix products, arithmetic and copies ran while one was open for 12% -> 0% of each run, Pallas kernels for 0% -> 0%
where the time goes in v1:
time: 340 us
  Pallas kernels  311 us (91%)
  other arithmetic  17.2 us (5%)
  local copies, waits for them, and re-layouts  10.8 us (3%)
    pallas_call x1, Pallas kernels, fused(): pl.pallas_call(functools.partial(kernel, sizes), out_shape=(jax.ShapeDtyp...  311 us

profile of v1, /device:TPU:0, one launch (start us, length us, event | category | flops | bytes accessed | tf_op | source)
XLA Modules:
  0.0 339.9 jit_solution(6629189912396155545)
XLA Ops:
  0.7 0.0 copy-start.3
  0.7 0.0 copy-start.2
  0.7 0.8 convert.110
  1.5 0.7 convert.111
  2.1 0.7 convert_element_type.46
  2.8 0.7 convert_bitcast_fusion.14
  3.5 0.7 convert_bitcast_fusion.12
  4.2 0.7 convert_bitcast_fusion.10
  4.8 0.7 convert_bitcast_fusion.2
  5.5 0.7 convert_bitcast_fusion.8
  6.2 0.7 convert_bitcast_fusion.6
  6.9 0.7 convert_bitcast_fusion.4
  7.5 0.1 stack.141
  7.6 0.7 fusion.3.small_ref
  8.3 1.0 copy.56
  9.3 0.0 copy-start.4
  9.3 1.0 copy.57
  10.3 1.0 convert.94
  11.3 0.0 copy-start.5
  11.3 1.0 convert.96
  12.4 0.0 copy-start.6
  12.4 0.0 copy-done.2
  12.4 0.9 multiply_convert_fusion.g_ref
  13.3 0.8 maximum_dynamic-update-slice_fusion.1
  14.0 0.0 copy-done.3
  14.1 0.7 bitcast_dynamic-update-slice_fusion.3
  14.7 0.0 copy-done.4
  14.7 0.7 bitcast_dynamic-update-slice_fusion.1
  15.4 0.8 maximum_dynamic-update-slice_fusion
  16.1 0.0 copy-done.5
  16.2 0.7 bitcast_dynamic-update-slice_fusion.2
  16.8 0.0 copy-done.6
  16.8 0.7 bitcast_dynamic-update-slice_fusion.ws_ref
  17.5 311.1 %two_blocks.1 = (f32[256,768]{1,0:T(8,128)}, f32[256,768]{1,0:T(8,128)}, f32[6,96,768]{2,1,0:T(8,128)}, f32[2,16,128]{2,1,0:T(8,128)}) custom-call(f32[256,768]{1,0:T(8,128)} %x_ref.1, bf16[256,768]{1,0:T(8,128)(2,1)} %multiply_convert_fusion.g_ref, bf16[6,96,768]{2,1,0:T(8,128)(2,1)} %bitcast_dynamic-update-slice_fusion.ws_ref, ...), custom_call_target="tpu_custom_call" | custom-call | tf_op jit(solution)/shard_map/two_blocks/pallas_call | solution.py:859
  328.6 1.3 slice_bitcast_fusion.21
  329.8 1.5 slice_bitcast_fusion.20
  331.4 0.6 pad_maximum_fusion.3
  332.0 0.6 pad_maximum_fusion.2
  332.5 2.4 slice_bitcast_fusion
  335.0 0.1 slice_bitcast_fusion.6
  335.1 0.7 copy.59
  335.8 0.7 pad_maximum_fusion.1
  336.6 0.1 slice_bitcast_fusion.10
  336.7 0.7 copy.58
  337.4 0.7 pad_maximum_fusion
  338.2 0.9 copy.67
  339.0 0.0 copy-done
  339.0 0.9 copy.68
  (6 shorter events, 0.0 us)
Async XLA Ops:
  0.7 13.4 %copy-start.3 = (f32[96,768]{1,0:T(8,128)S(1)}, f32[96,768]{1,0:T(8,128)}, u32[]{:S(2)}) copy-start(f32[96,768]{1,0:T(8,128)} %param.41) | copy-start | bytes 884740
  0.7 11.7 %copy-start.2 = (f32[256,768]{1,0:T(8,128)S(1)}, f32[256,768]{1,0:T(8,128)}, u32[]{:S(2)}) copy-start(f32[256,768]{1,0:T(8,128)} %param.31) | copy-start | bytes 2359300
  9.3 5.4 %copy-start.4 = (f32[768,96]{0,1:T(8,128)S(1)}, f32[768,96]{0,1:T(8,128)}, u32[]{:S(2)}) copy-start(f32[768,96]{0,1:T(8,128)} %param.43) | copy-start | bytes 884740
  11.3 4.8 %copy-start.5 = (f32[96,768]{1,0:T(8,128)S(1)}, f32[96,768]{1,0:T(8,128)}, u32[]{:S(2)}) copy-start(f32[96,768]{1,0:T(8,128)} %param.53) | copy-start | bytes 884740
  12.4 4.5 %copy-start.6 = (f32[768,96]{0,1:T(8,128)S(1)}, f32[768,96]{0,1:T(8,128)}, u32[]{:S(2)}) copy-start(f32[768,96]{0,1:T(8,128)} %param.55) | copy-start | bytes 884740
  335.0 3.2 copy-start.1
  335.8 3.2 copy-start

commit v2 on v1

v2 whole, which is shorter than its diff:
```python
import functools

import jax
import jax.numpy as jnp
import numpy as np
from jax import lax
from jax.experimental import pallas as pl
from jax.experimental.pallas import tpu as pltpu
from jax.sharding import PartitionSpec as P

MESH = pl.DeviceIdType.MESH
HEAD = 64
SIDE = 16
TUBE = 4
FRAME = SIDE * SIDE
CLIP = 4096
EPS = 1e-06
INNER = 8
LEAD = 3
LAG = 3
DEPTH = 3
LAG_TWO = 4
LAG_THREE = 7
F32 = jnp.float32
BF16 = jnp.bfloat16


def mm(left, right):
    return lax.dot_general(left, right, (((1,), (0,)), ((), ())), preferred_element_type=F32)


def mm_t(left, right):
    return lax.dot_general(left, right, (((1,), (1,)), ((), ())), preferred_element_type=F32)


def t_mm(left, right):
    return lax.dot_general(left, right, (((0,), (0,)), ((), ())), preferred_element_type=F32)


def exact(left, right, dims):
    return lax.dot_general(
        left, right, (dims, ((), ())), precision=lax.Precision.HIGHEST, preferred_element_type=F32
    )


def flip(value, weight):
    bit = (value // weight) % 2
    return value + weight * (1 - 2 * bit)


def flip_by(value, key):
    weight = 1
    while key:
        if key & 1:
            value = flip(value, weight)
        key >>= 1
        weight *= 2
    return value


def unit_rows(values):
    center = values - jnp.mean(values, axis=-1, keepdims=True)
    spread = jnp.mean(center * center, axis=-1, keepdims=True)
    scale = lax.rsqrt(spread + EPS)
    return center * scale, scale


def kernel(
    sizes,
    count,
    *refs,
):
    x_ref, ct_ref, bits_ref = refs[:3]
    matrices = (refs[3:7], refs[7:11])
    vectors = refs[11:11 + count]
    swap_ref, tiles_ref, mask_ref, out_ref, ig_ref = refs[11 + count:16 + count]
    grads_out = (refs[16 + count:20 + count], refs[20 + count:24 + count])
    sg_ref = refs[24 + count]
    body(
        sizes, x_ref, ct_ref, bits_ref, matrices, vectors, swap_ref, tiles_ref, mask_ref, out_ref, ig_ref,
        grads_out, sg_ref, *refs[25 + count:]
    )


def body(
    sizes,
    x_ref,
    ct_ref,
    bits_ref,
    matrices,
    vectors,
    swap_ref,
    tiles_ref,
    mask_ref,
    out_ref,
    ig_ref,
    grads_out,
    sg_ref,
    W,
    SG,
    SV,
    BI,
    BU,
    H,
    M,
    NB,
    NT,
    GT,
    PK,
    CT,
    HID,
    GP,
    PR,
    ACC,
    GR,
    SGR,
    XS,
    XR,
    SB,
    RB,
    HS,
    CS,
    US,
    PS,
    LS,
    zs,
    zr,
    h1s,
    h1r,
    h2s,
    h2r,
    cs,
    cr,
    vs,
    vr,
    ts,
    tr,
    ss,
    sr,
    rs,
    rr,
    free,
    free_c,
    WI,
    WO,
    SM,
    ls,
):
    outer, nmp, d, rows = sizes
    per = INNER
    half = d // 2
    dp = lax.axis_index("dp")
    z = lax.axis_index("mp")
    low = dp % outer
    q = dp // outer
    c = q % 2
    x = (q // 2) % 2
    y = q // 4
    oc, ox, oy = 1 - c, 1 - x, 1 - y
    members = CLIP // FRAME
    dpc = members // nmp
    me = (dp % dpc) * nmp + z

    def place(cc, xx, yy):
        return (yy * 4 + xx * 2 + cc) * outer + low

    to_c = (place(oc, x, y), z)
    to_x = (place(c, ox, y), z)
    to_y = (place(c, x, oy), z)

    def to_z(zz):
        return (dp, zz)

    def peer(key):
        return flip_by(q, key // nmp), flip_by(z, key % nmp)

    def to_peer(key):
        qq, zz = peer(key)
        return (qq * outer + low, zz)

    def to_member(f):
        return ((dp // dpc) * dpc + f // nmp, f % nmp)

    def send(src, dst, s_sem, r_sem, device):
        pltpu.make_async_remote_copy(
            src_ref=src, dst_ref=dst, send_sem=s_sem, recv_sem=r_sem, device_id=device, device_id_type=MESH
        ).start()

    def sent(src, s_sem):
        pltpu.make_async_remote_copy(
            src_ref=src, dst_ref=src, send_sem=s_sem, recv_sem=s_sem, device_id=to_c, device_id_type=MESH
        ).wait_send()

    def got(dst, r_sem):
        pltpu.make_async_remote_copy(
            src_ref=dst, dst_ref=dst, send_sem=r_sem, recv_sem=r_sem, device_id=to_c, device_id_type=MESH
        ).wait_recv()

    def keep(src, dst, n):
        return pltpu.make_async_copy(src, dst, ls.at[n])

    block = d // per
    third = d // nmp

    def matrix_copies(b):
        inw, outw, up, down = matrices[b]
        return (
            keep(inw, WI.at[b], 4 * b),
            keep(outw, WO.at[b], 4 * b + 1),
            keep(up, M.at[b, pl.ds(0, block)], 4 * b + 2),
            keep(down, M.at[b, pl.ds(block, block)], 4 * b + 3),
        )

    for b in range(2):
        for copy in matrix_copies(b):
            copy.start()
    keep(x_ref, ACC, 8).start()
    keep(ct_ref, GR, 9).start()

    barrier = pltpu.get_barrier_semaphore()
    greeted = [to_peer(key) for key in range(1, nmp * per)]
    if outer > 1:
        greeted += [to_member(flip_by(me, key)) for key in range(1, members)]
    for device in greeted:
        pl.semaphore_signal(barrier, inc=1, device_id=device, device_id_type=MESH)
    SM[...] = jnp.zeros_like(SM)
    narrow = 0
    for i, ref in enumerate(vectors[:12]):
        narrow = ref.shape[1]
        SM[i:i + 1, 0:narrow] = ref[...]
    for i, ref in enumerate(vectors[12:14]):
        SM[12 + 2 * i:14 + 2 * i, 0:narrow] = ref[...]
    for i, ref in enumerate(vectors[14:16]):
        SM[i:i + 1, 32:32 + ref.shape[1]] = ref[...]
    SG[z, y, x, c] = SM[...].astype(BF16)

    def own_shards(b):
        copies = matrix_copies(b)
        copies[0].wait()
        copies[1].wait()
        parts = [WI[b, 0], WI[b, 2], WI[b, 1], WO[b].T]
        W[3 * b, z, y, x, c] = jnp.concatenate(parts, axis=1).astype(BF16)
        copies[2].wait()
        W[3 * b + 1, z, y, x, c] = M[b, 0:block].astype(BF16)
        copies[3].wait()
        W[3 * b + 2, z, y, x, c] = M[b, block:2 * block].astype(BF16)

    own_shards(0)
    pl.semaphore_wait(barrier, len(greeted))

    def z_start(m):
        for key in range(1, nmp):
            ref = W.at[m, z, y, x, c]
            send(ref, ref, zs.at[m], zr.at[m, z], to_z(flip_by(z, key)))

    def g1(m, k):
        zz = flip_by(z, k)
        if k:
            got(W.at[m, zz, y, x, c], zr.at[m, zz])
        t = m * nmp + k
        left = W.at[m, zz, y, x, c, :, pl.ds(0, half)]
        right = W.at[m, zz, y, x, c, :, pl.ds(half, half)]
        send(left, left, h1s.at[m], h1r.at[t], to_x)
        send(right, right, h1s.at[m], h1r.at[t], to_y)

    def g2(m, k):
        zz = flip_by(z, k)
        t = m * nmp + k
        got(W.at[m, zz, oy, ox, c], h1r.at[t])
        left = W.at[m, zz, y, :, c, :, pl.ds(0, half)]
        right = W.at[m, zz, :, x, c, :, pl.ds(half, half)]
        send(left, left, h2s.at[m], h2r.at[t], to_y)
        send(right, right, h2s.at[m], h2r.at[t], to_x)

    def g3(m, k):
        zz = flip_by(z, k)
        t = m * nmp + k
        got(W.at[m, zz, oy, :, c], h2r.at[t])
        whole = W.at[m, zz, :, :, c]
        send(whole, whole, cs.at[m], cr.at[t], to_c)

    def g4(m, k):
        zz = flip_by(z, k)
        t = m * nmp + k
        got(W.at[m, zz, :, :, oc], cr.at[t])

    def g_done(m):
        sent(W.at[m, pl.ds(0, nmp - 1), y, x, c], zs.at[m])
        sent(W.at[m, :, y, x, c], h1s.at[m])
        sent(W.at[m, :, y, :, c], h2s.at[m])
        sent(W.at[m, :, :, :, c], cs.at[m])

    total = 6 * nmp

    def advance(t, base=0):
        def ranged(s, stage):
            if s < 0:
                return
            m, k = s, 0
            if s >= LEAD:
                m, k = (s - LEAD) // nmp, (s - LEAD) % nmp
                if k == 0:
                    m += LEAD
            if m < 3 or (m < 6 and isinstance(base, int)):
                stage(base + m, k)
            elif m < 6:
                pl.when(base == 0)(lambda: stage(m, k))

        def first(m, k):
            if k == 1:
                if isinstance(m, int):
                    if m + 1 < 6:
                        z_start(m + 1)
                else:
                    pl.when(m + 1 < 6)(lambda: z_start(m + 1))
            g1(m, k)

        ranged(t - LAG, g2)
        ranged(t, first)
        ranged(t - LAG - DEPTH, g3)
        ranged(t - LAG - DEPTH - 1, g4)

    def complete(j):
        return nmp * (j + 1) + LEAD + LAG + DEPTH

    def release(m):
        g_done(m)
        for device in [to_x, to_y] + [to_z(flip_by(z, key)) for key in range(1, nmp)]:
            pl.semaphore_signal(free.at[m], inc=1, device_id=device, device_id_type=MESH)

    def may_send(m):
        pl.semaphore_wait(free.at[m], nmp + 1)

    def r1(m, k):
        t = m * nmp + k
        send(
            W.at[m, k, :, ox, c, :, pl.ds(0, half)],
            W.at[m, k, :, ox, oc, :, pl.ds(0, half)],
            h2s.at[m],
            h2r.at[t],
            to_x,
        )
        send(
            W.at[m, k, oy, :, c, :, pl.ds(half, half)],
            W.at[m, k, oy, :, oc, :, pl.ds(half, half)],
            h2s.at[m],
            h2r.at[t],
            to_y,
        )

    def add_to(dst, src):
        dst[...] = (dst[...].astype(F32) + src[...].astype(F32)).astype(BF16)

    def r2(m, k):
        t = m * nmp + k
        got(W.at[m, k, y, :, oc], h2r.at[t])
        add_to(W.at[m, k, :, x, c, :, pl.ds(0, half)], W.at[m, k, :, x, oc, :, pl.ds(0, half)])
        send(
            W.at[m, k, oy, x, c, :, pl.ds(0, half)],
            W.at[m, k, oy, ox, oc, :, pl.ds(0, half)],
            h1s.at[m],
            h1r.at[t],
            to_y,
        )
        add_to(W.at[m, k, y, :, c, :, pl.ds(half, half)], W.at[m, k, y, :, oc, :, pl.ds(half, half)])
        send(
            W.at[m, k, y, ox, c, :, pl.ds(half, half)],
            W.at[m, k, oy, ox, oc, :, pl.ds(half, half)],
            h1s.at[m],
            h1r.at[t],
            to_x,
        )

    def r3(m, k):
        t = m * nmp + k
        got(W.at[m, k, y, x, oc], h1r.at[t])
        add_to(W.at[m, k, y, x, c, :, pl.ds(0, half)], W.at[m, k, y, ox, oc, :, pl.ds(0, half)])
        add_to(W.at[m, k, y, x, c, :, pl.ds(half, half)], W.at[m, k, oy, x, oc, :, pl.ds(half, half)])

        @pl.when(k != z)
        def _():
            send(W.at[m, k, y, x, c], W.at[m, z, oy, ox, oc], zs.at[m], zr.at[m, z], to_z(k))

    def r4(m):
        sum_ = W[m, z, y, x, c].astype(F32)
        for key in range(1, nmp):
            zz = flip_by(z, key)
            src = W.at[m, zz, oy, ox, oc]
            got(src, zr.at[m, zz])
            sum_ = sum_ + src[...].astype(F32)
        b, j = m // 3, m % 3
        if j == 0:
            WI[b, 0] = sum_[:, 0:third]
            WI[b, 2] = sum_[:, third:2 * third]
            WI[b, 1] = sum_[:, 2 * third:3 * third]
            WO[b] = sum_[:, 3 * third:].T
            result_copy(b, 0).start()
            result_copy(b, 1).start()
        else:
            M[b, (j - 1) * block:j * block] = sum_
            result_copy(b, j + 1).start()

    def result_copy(b, i):
        src = (WI.at[b], WO.at[b], M.at[b, pl.ds(0, block)], M.at[b, pl.ds(block, block)])[i]
        return keep(src, grads_out[b][i], 4 * b + i)

    def r_done(m):
        sent(W.at[m, pl.ds(0, nmp - 1), y, x, c], zs.at[m])
        sent(W.at[m, :, y, x, c], h1s.at[m])
        sent(W.at[m, :, y, :, c], h2s.at[m])

    def chunk(k):
        key, out, weight = nmp - 1 - k, 0, 1
        while weight < nmp:
            out = out + weight * ((z // weight + key // weight) % 2)
            weight *= 2
        return out

    def retreat(u):
        def at(s, stage):
            stage(5 - s // nmp, chunk(s % nmp))

        if isinstance(u, int):
            if u < total:
                at(u, r1)
            if u - LAG_TWO < total:
                at(u - LAG_TWO, r2)
            if u - LAG_THREE < total:
                at(u - LAG_THREE, r3)
            return
        at(u, r1)
        pl.when(u >= LAG_TWO)(lambda: at(u - LAG_TWO, r2))
        pl.when(u >= LAG_THREE)(lambda: at(u - LAG_THREE, r3))

    def swap_start(i):
        RB[i, pl.ds(me, 1)] = SB[i, pl.ds(me, 1)]
        for key in range(1, members):
            f = flip_by(me, key)
            send(SB.at[i, f], RB.at[i, me], ts.at[i], tr.at[i], to_member(f))

    def swap_wait(i):
        got(RB.at[i, pl.ds(0, members - 1)], tr.at[i])

    def swap_done(i):
        sent(SB.at[i, pl.ds(0, members - 1)], ts.at[i])

    def rows_of(ref, i):
        return ref[i].reshape(rows, d)

    for key in range(1, nmp):
        ref = SG.at[z, y, x, c]
        send(ref, ref, vs.at[0], vr.at[0], to_z(flip_by(z, key)))
    z_start(0)
    advance(0)
    advance(1)
    own_shards(1)
    got(SG.at[pl.ds(0, nmp - 1), y, x, c], vr.at[0])
    ref = SG.at[:, y, x, c]
    send(ref, ref, vs.at[1], vr.at[1], to_x)
    swap = swap_ref[...]
    keep(x_ref, ACC, 8).wait()
    H[0] = exact(swap.astype(F32), ACC[...], ((1,), (0,)))
    advance(2)
    got(SG.at[:, y, ox, c], vr.at[1])
    ref = SG.at[:, y, :, c]
    send(ref, ref, vs.at[2], vr.at[2], to_y)
    advance(3)
    got(SG.at[:, oy, :, c], vr.at[2])
    ref = SG.at[:, :, :, c]
    send(ref, ref, vs.at[3], vr.at[3], to_c)
    advance(4)
    got(SG.at[:, :, :, oc], vr.at[3])

    lane = lax.broadcasted_iota(jnp.int32, (1, d), 1)
    tall = SG[...].reshape(nmp * per * 16, 128)
    spread = mm(tall, tiles_ref[0]).reshape(nmp * per, 16, d)
    spread = jnp.sum(spread * mask_ref[0:nmp * per].reshape(nmp * per, 1, d), axis=0)
    SV[0, 0:6] = spread[0:6]
    SV[1, 0:6] = spread[6:12]
    is_q = (lane < third).astype(F32)
    is_v = jnp.logical_and(lane >= third, lane < 2 * third).astype(F32)
    spread_in = mm(tall, tiles_ref[1]).reshape(nmp, per, 16, d)
    spread_up = mm(tall, tiles_ref[2]).reshape(nmp, per, 16, d)
    mask_in = mask_ref[nmp * per:nmp * per + per].reshape(per, 1, d)
    mask_up = mask_ref[nmp * per + per:nmp * per + 2 * per].reshape(per, 1, d)
    for k in range(nmp):
        one = jnp.sum(spread_in[k] * mask_in, axis=0)
        two = jnp.sum(spread_up[k] * mask_up, axis=0)
        for b in range(2):
            BI[b, k] = one[12 + 2 * b:13 + 2 * b] * is_q + one[13 + 2 * b:14 + 2 * b] * is_v
            BU[b, k] = two[b:b + 1]
    for t in range(5, complete(0) + 1):
        advance(t)

    lane2 = lax.broadcasted_iota(jnp.int32, (1, 256), 1)
    heads = third // HEAD

    def head_mask(lead):
        return jnp.logical_and(lane2 >= lead * HEAD, lane2 < lead * HEAD + HEAD).astype(F32).astype(BF16)

    q_masks = [head_mask(h) for h in range(heads)]
    v_masks = [head_mask(h + 1) for h in range(heads)]
    scale = HEAD ** (-0.5)
    wide = 5 * 128

    def flat(values):
        return values.reshape(d, values.shape[-1])

    def lower(values):
        return values.reshape(half, values.shape[-1])

    def tall_view(values):
        return values.T.astype(BF16).reshape(2, 2, 2, d // per, rows)

    def to_sibling(src, dst, n):
        send(src, dst, ss.at[n], sr.at[n], to_c)

    def early_to_sibling(b):
        to_sibling(HID.at[b], HS, 0)
        to_sibling(NT.at[b, 0, :, :, oc], LS.at[0], 1)
        to_sibling(NT.at[b, 1, :, :, oc], LS.at[1], 2)
        to_sibling(CT.at[b], CS, 3)

    def take_grad(b):
        grad = GR[...]
        SGR[pl.ds(16 * b + 5, 1)] = jnp.sum(grad, axis=0, keepdims=True)
        NB[...] = grad.astype(BF16)
        GT[0] = tall_view(grad)
        to_sibling(GT.at[0, :, :, oc], LS.at[2], 4)

    def shrink(b, k):
        hidden_grad = mm(NB[...], flat(W[3 * b + 2, k]))
        upper_grad = (GP[b, k].astype(F32) * hidden_grad).astype(BF16)
        GP[b, k] = upper_grad
        to_sibling(GP.at[b, k], US.at[k], 6)
        SGR[pl.ds(16 * b + 10 + k, 1)] = jnp.sum(upper_grad.astype(F32), axis=0, keepdims=True)

    def forward(b, _):
        m = 3 * b
        h = H[b]
        unit, _s = unit_rows(h)
        normed = unit * SV[b, 0:1] + SV[b, 1:2]
        NB[...] = normed.astype(BF16)
        NT[b, 0] = tall_view(normed)
        ACC[...] = h + SV[b, 2:3]

        def attend(k, _):
            packed = (mm(NB[...], flat(W[m, k, :, :, :, :, 0:wide])) + BI[b, k, :, 0:wide]).astype(BF16)
            PK[b, k] = packed
            qs = packed[:, 0:256] * BF16(scale)
            vv = packed[:, 128:384]
            kk = packed[:, 384:640]
            mixed = jnp.zeros((rows, 256), F32)
            for h in range(heads):
                scores = mm_t(qs * q_masks[h], kk)
                expo = jnp.exp(scores - jnp.max(scores, axis=-1, keepdims=True))
                probs = (expo * (1.0 / jnp.sum(expo, axis=-1, keepdims=True))).astype(BF16)
                PR[b, k, h] = probs
                mixed += mm(probs, vv * v_masks[h])
            mixed = mixed.astype(BF16)
            CT[b, k] = mixed
            ACC[...] += mm_t(mixed, flat(W[m, k, :, :, :, :, d - 256:d]))
            return 0

        lax.fori_loop(0, nmp, attend, 0)
        for t in range(complete(0) + 1, complete(1) + 1):
            advance(t, m)
        middle = ACC[...]
        M[b] = middle
        unit, _s = unit_rows(middle)
        normed = unit * SV[b, 3:4] + SV[b, 4:5]
        NB[...] = normed.astype(BF16)
        NT[b, 1] = tall_view(normed)
        ACC[...] = middle + SV[b, 5:6]

        def expand(k, _):
            upper = mm(NB[...], flat(W[m + 1, k])) + BU[b, k]
            cdf = 0.5 + 0.5 * lax.erf(upper * (0.5 ** 0.5))
            HID[b, k] = (upper * cdf).astype(BF16)
            density = jnp.exp(-0.5 * upper * upper) * ((2 * np.pi) ** -0.5)
            GP[b, k] = (cdf + upper * density).astype(BF16)
            return 0

        lax.fori_loop(0, nmp, expand, 0)

        @pl.when(b == 0)
        def _():
            keep(ct_ref, GR, 9).wait()
            picked = (swap.astype(F32) * bits_ref[...].astype(F32)).astype(BF16)
            SB[0] = mm(picked, GR[...].astype(BF16)).astype(BF16).reshape(members, rows // members, d)
            swap_start(0)

        @pl.when(b == 1)
        def _():
            early_to_sibling(1)
            swap_wait(0)
            GR[...] = rows_of(RB, 0).astype(F32)
            take_grad(1)

        def contract(k):
            pl.when(b == 1)(lambda: shrink(1, k))
            ACC[...] += mm_t(HID[b, k], flat(W[m + 2, k]))

        contract(z)
        for t in range(complete(1) + 1, complete(2) + 1):
            advance(t, m)
            if t > complete(2) - nmp + 1:
                contract(flip_by(z, t - complete(2) + nmp - 1))
        SB[1 + b] = ACC[...].astype(BF16).reshape(members, rows // members, d)
        swap_start(1 + b)
        for t in range(complete(2) + 1, complete(3) + 1):
            advance(t, m)

        @pl.when(b == 0)
        def _():
            swap_wait(1)
            H[1] = rows_of(RB, 1).astype(F32)
        return 0

    lax.fori_loop(0, 2, forward, 0)

    def norm_back(grad, start, gain):
        unit, scale = unit_rows(start)
        lifted = grad * gain
        back = scale * (
            lifted
            - jnp.mean(lifted, axis=-1, keepdims=True)
            - unit * jnp.mean(lifted * unit, axis=-1, keepdims=True)
        )
        return back, jnp.sum(grad * unit, axis=0, keepdims=True), jnp.sum(grad, axis=0, keepdims=True)

    def deal():
        rows_ = []
        for zz in range(nmp):
            own = mask_ref[zz * per:zz * per + per].reshape(per, 1, d)
            plain = jnp.concatenate([SGR[0:6], SGR[16:22]], axis=0).reshape(1, 12, d) * own
            pair = jnp.concatenate([SGR[6 + zz:7 + zz], SGR[22 + zz:23 + zz]], axis=0).reshape(1, 2, d) * mask_in
            up = jnp.concatenate([SGR[10 + zz:11 + zz], SGR[26 + zz:27 + zz]], axis=0).reshape(1, 2, d) * mask_up
            rows_ = jnp.concatenate([plain, pair, up], axis=1).reshape(per * 16, d)
            high = rows_.astype(BF16)
            rest = (rows_ - high.astype(F32)).astype(BF16)
            line = lax.broadcasted_iota(jnp.int32, (per, 16, 128), 1)
            parts = [
                (mm_t(high, tiles_ref[i]) + mm_t(rest, tiles_ref[i])).reshape(per, 16, 128) for i in (0, 3, 2)
            ]
            XS[zz] = jnp.where(line < 12, parts[0], jnp.where(line < 14, parts[1], parts[2]))
        for key in range(1, nmp * per):
            qq, zz = peer(key)
            send(XS.at[zz, qq], XR.at[key], rs.at[0], rr.at[0], to_peer(key))

    def backward(step, _):
        b = 1 - step
        m = 3 * b
        row = 16 * b

        @pl.when(step == 1)
        def _():
            pl.semaphore_wait(free_c, 1)
            early_to_sibling(b)
            take_grad(b)

            def shrink_all(k, _):
                shrink(b, k)
                return 0

            lax.fori_loop(0, nmp, shrink_all, 0)

        release(m + 2)
        got(HS, sr.at[0])
        got(LS.at[2], sr.at[4])
        may_send(m + 2)

        def down_grad(step_k, _):
            k = chunk(step_k)
            own = mm(lower(GT[0, :, :, c]), HID[b, k]) + mm(lower(LS[2]), HS[k])
            W[m + 2, k, :, :, c] = own.astype(BF16).reshape(2, 2, d // per, d)
            retreat(3 * nmp * step + step_k)
            return 0

        lax.fori_loop(0, nmp, down_grad, 0)
        pl.when(step == 1)(lambda: r4(5))
        ACC[...] = jnp.zeros_like(ACC)

        def spread_up(k, _):
            ACC[...] += mm_t(GP[b, k], flat(W[m + 1, k]))
            return 0

        lax.fori_loop(0, nmp, spread_up, 0)
        release(m + 1)
        got(US, sr.at[6])
        got(LS.at[1], sr.at[2])
        may_send(m + 1)

        def up_grad(step_k, _):
            k = chunk(step_k)
            own = mm(lower(NT[b, 1, :, :, c]), GP[b, k]) + mm(lower(LS[1]), US[k])
            W[m + 1, k, :, :, c] = own.astype(BF16).reshape(2, 2, d // per, d)
            retreat(3 * nmp * step + nmp + step_k)
            return 0

        lax.fori_loop(0, nmp, up_grad, 0)
        pl.when(step == 1)(lambda: r4(4))
        back, gain_grad, bias_grad = norm_back(ACC[...], M[b], SV[b, 3:4])
        SGR[pl.ds(row + 3, 1)] = gain_grad
        SGR[pl.ds(row + 4, 1)] = bias_grad
        middle_grad = GR[...] + back
        GR[...] = middle_grad
        SGR[pl.ds(row + 2, 1)] = jnp.sum(middle_grad, axis=0, keepdims=True)
        NB[...] = middle_grad.astype(BF16)
        GT[1] = tall_view(middle_grad)
        to_sibling(GT.at[1, :, :, oc], LS.at[3], 5)
        ACC[...] = jnp.zeros_like(ACC)
        def attend_back(k, _):
            mixed_grad = mm(NB[...], flat(W[m, k, :, :, :, :, d - 256:d])).astype(BF16)
            packed = PK[b, k]
            qs = packed[:, 0:256] * BF16(scale)
            vv = packed[:, 128:384]
            kk = packed[:, 384:640]
            q_grad = jnp.zeros((rows, 256), F32)
            k_grad = jnp.zeros((rows, 256), F32)
            v_grad = jnp.zeros((rows, 256), F32)
            for h in range(heads):
                part = mixed_grad * v_masks[h]
                probs_low = PR[b, k, h]
                probs = probs_low.astype(F32)
                weighted = probs * mm_t(part, vv)
                score_grad = (weighted - probs * jnp.sum(weighted, axis=-1, keepdims=True)).astype(BF16)
                q_grad += mm(score_grad, kk * q_masks[h])
                k_grad += t_mm(score_grad, qs * q_masks[h])
                v_grad += t_mm(probs_low, part)
            q_grad = q_grad * scale
            packed_grad = jnp.concatenate(
                [q_grad[:, 0:128], q_grad[:, 128:256] + v_grad[:, 0:128], v_grad[:, 128:256], k_grad], axis=1
            ).astype(BF16)
            PK[b, k] = packed_grad
            to_sibling(PK.at[b, k], PS.at[k], 7)
            SGR[pl.ds(row + 6 + k, 1), 0:wide] = jnp.sum(packed_grad.astype(F32), axis=0, keepdims=True)
            ACC[...] += mm_t(packed_grad, flat(W[m, k, :, :, :, :, 0:wide]))
            return 0

        lax.fori_loop(0, nmp, attend_back, 0)
        release(m)
        back, gain_grad, bias_grad = norm_back(ACC[...], H[b], SV[b, 0:1])
        SGR[pl.ds(row, 1)] = gain_grad
        SGR[pl.ds(row + 1, 1)] = bias_grad
        GR[...] = GR[...] + back

        @pl.when(step == 0)
        def _():
            SB[3] = GR[...].astype(BF16).reshape(members, rows // members, d)
            swap_start(3)

        pl.when(step == 1)(deal)
        got(PS, sr.at[7])
        got(LS.at[0], sr.at[1])
        got(LS.at[3], sr.at[5])
        got(CS, sr.at[3])
        may_send(m)

        def in_grad(step_k, _):
            k = chunk(step_k)
            one = mm(lower(NT[b, 0, :, :, c]), PK[b, k]) + mm(lower(LS[0]), PS[k])
            two = mm(lower(GT[1, :, :, c]), CT[b, k]) + mm(lower(LS[3]), CS[k])
            own = jnp.concatenate(
                [one[:, 0:512], one[:, 512:640] + two[:, 0:128], two[:, 128:256]], axis=1
            ).astype(BF16)
            W[m, k, :, :, c] = own.reshape(2, 2, d // per, d)
            retreat(3 * nmp * step + 2 * nmp + step_k)
            return 0

        lax.fori_loop(0, nmp, in_grad, 0)

        sent(HID.at[b], ss.at[0])
        sent(NT.at[b, 0, :, :, oc], ss.at[1])
        sent(NT.at[b, 1, :, :, oc], ss.at[2])
        sent(CT.at[b], ss.at[3])
        sent(GT.at[0, :, :, oc], ss.at[4])
        sent(GT.at[1, :, :, oc], ss.at[5])
        sent(GP.at[b], ss.at[6])
        sent(PK.at[b], ss.at[7])

        @pl.when(step == 0)
        def _():
            pl.semaphore_signal(free_c, inc=1, device_id=to_c, device_id_type=MESH)

        pl.when(step == 1)(lambda: r4(3))

        @pl.when(step == 0)
        def _():
            swap_wait(3)
            GR[...] = rows_of(RB, 3).astype(F32)
        return 0

    lax.fori_loop(0, 2, backward, 0)

    swap_wait(2)
    H[1] = mm(swap, rows_of(RB, 2))
    keep(H.at[1], out_ref, 8).start()
    ACC[...] = exact(swap.astype(F32), GR[...], ((1,), (0,)))
    keep(ACC, ig_ref, 9).start()
    for u in range(total, total + LAG_THREE):
        retreat(u)
    r4(2)
    got(XR.at[pl.ds(1, nmp * per - 1)], rr.at[0])
    sg_ref[...] = XS[z, q] + jnp.sum(XR[1:nmp * per], axis=0)
    r4(1)
    r4(0)
    sent(XR.at[pl.ds(1, nmp * per - 1)], rs.at[0])
    for b in range(2):
        for i in range(4):
            result_copy(b, i).wait()
    keep(H.at[1], out_ref, 8).wait()
    keep(ACC, ig_ref, 9).wait()
    for m in range(6):
        r_done(m)
    for i in range(4):
        swap_done(i)
    sent(SG.at[pl.ds(0, nmp - 1), y, x, c], vs.at[0])
    sent(SG.at[:, y, x, c], vs.at[1])
    sent(SG.at[:, y, :, c], vs.at[2])
    sent(SG.at[:, :, :, c], vs.at[3])


def tables(outer, ndp, nmp, d):
    n = d // (ndp * nmp)
    tiles = np.zeros((4, 128, d), np.float32)
    masks = np.zeros((nmp * INNER + 2 * INNER, d), np.float32)
    for at in range(d):
        i = at % n
        zz = (at // n) % nmp
        pp = at // (n * nmp)
        qq, lo = pp // outer, pp % outer
        tiles[0, lo * n + i, at] = 1
        masks[zz * INNER + qq, at] = 1
    third = d // nmp
    step = third // INNER
    for at in range(2 * third):
        tiles[1, at % step, at] = 1
        tiles[3, at % step + 32 * (at // third), at] = 1
        masks[nmp * INNER + (at % third) // step, at] = 1
    step = d // INNER
    for at in range(d):
        tiles[2, 32 + at % step, at] = 1
        masks[nmp * INNER + INNER + at // step, at] = 1
    return tiles, masks


def turn_table():
    swap = np.zeros((FRAME, FRAME), np.float32)
    across = SIDE // TUBE
    for wr in range(across):
        for i in range(TUBE):
            for wc in range(across):
                for j in range(TUBE):
                    natural = ((wr * TUBE + i) * across + wc) * TUBE + j
                    turned = ((wr * across + wc) * TUBE + i) * TUBE + j
                    swap[turned, natural] = 1
    return swap


def fused(sizes, x, cotangent, bits, matrices, vectors, ndp):
    outer, nmp, d, rows = sizes
    tiles, masks = tables(outer, ndp, nmp, d)
    members = CLIP // FRAME
    vmem = pltpu.VMEM
    dma = pltpu.SemaphoreType.DMA
    regular = pltpu.SemaphoreType.REGULAR
    block = d // INNER
    steps = 6 * nmp
    scratch = [
        vmem((6, nmp, 2, 2, 2, block, d), BF16),
        vmem((nmp, 2, 2, 2, 16, 128), BF16),
        vmem((2, 8, d), F32),
        vmem((2, nmp, 1, d), F32),
        vmem((2, nmp, 1, d), F32),
        vmem((2, rows, d), F32),
        vmem((2, rows, d), F32),
        vmem((rows, d), BF16),
        vmem((2, 2, 2, 2, 2, block, rows), BF16),
        vmem((2, 2, 2, 2, block, rows), BF16),
        vmem((2, nmp, rows, 640), BF16),
        vmem((2, nmp, rows, 256), BF16),
        vmem((2, nmp, rows, d), BF16),
        vmem((2, nmp, rows, d), BF16),
        vmem((2, nmp, d // nmp // HEAD, rows, rows), BF16),
        vmem((rows, d), F32),
        vmem((rows, d), F32),
        vmem((32, d), F32),
        vmem((nmp, INNER, 16, 128), F32),
        vmem((nmp * INNER, 16, 128), F32),
        vmem((4, members, rows // members, d), BF16),
        vmem((4, members, rows // members, d), BF16),
        vmem((nmp, rows, d), BF16),
        vmem((nmp, rows, 256), BF16),
        vmem((nmp, rows, d), BF16),
        vmem((nmp, rows, 640), BF16),
        vmem((4, 2, 2, block, rows), BF16),
        dma((6,)),
        dma((6, nmp)),
        dma((6,)),
        dma((steps,)),
        dma((6,)),
        dma((steps,)),
        dma((6,)),
        dma((steps,)),
        dma((4,)),
        dma((4,)),
        dma((4,)),
        dma((4,)),
        dma((8,)),
        dma((8,)),
        dma((1,)),
        dma((1,)),
        regular((6,)),
        regular,
        vmem((2, 3, block, d // nmp), F32),
        vmem((2, d // nmp, block), F32),
        vmem((16, 128), F32),
        dma((10,)),
    ]
    grads = [
        jax.ShapeDtypeStruct((3, block, d // nmp), F32),
        jax.ShapeDtypeStruct((d // nmp, block), F32),
        jax.ShapeDtypeStruct((block, d), F32),
        jax.ShapeDtypeStruct((block, d), F32),
    ]
    whole = jax.ShapeDtypeStruct((rows, d), F32)
    anywhere = pl.BlockSpec(memory_space=pl.ANY)
    inside = pl.BlockSpec(memory_space=vmem)
    return pl.pallas_call(
        functools.partial(kernel, sizes, len(vectors)),
        out_shape=[whole, whole] + grads + grads + [jax.ShapeDtypeStruct((16, 128), F32)],
        in_specs=[anywhere] * 2 + [inside] + [anywhere] * 8 + [inside] * (len(vectors) + 3),
        out_specs=[anywhere] * 10 + [inside],
        scratch_shapes=scratch,
        compiler_params=pltpu.CompilerParams(
            collective_id=0, has_side_effects=True, vmem_limit_bytes=64 << 20
        ),
        name="two_blocks",
    )(
        x,
        cotangent,
        bits,
        *matrices,
        *vectors,
        jnp.asarray(turn_table(), BF16),
        jnp.asarray(tiles, BF16),
        jnp.asarray(masks, F32),
    )


def settle_kernel(wide, *refs):
    big, sg_ref, outs = refs[:10], refs[10], refs[11:37]
    held, sems = refs[37:47], refs[47]
    copies = []
    for i in range(10):
        copies.append(
            (
                pltpu.make_async_copy(big[i], held[i], sems.at[0, i]),
                pltpu.make_async_copy(held[i], outs[i], sems.at[1, i]),
            )
        )
        copies[i][0].start()
    for b in range(2):
        small = outs[10 + 8 * b:18 + 8 * b]
        for i in range(6):
            small[i][...] = sg_ref[6 * b + i:6 * b + i + 1, 0:wide]
        small[6][0:1] = sg_ref[12 + b:13 + b, 0:wide]
        small[6][1:2] = sg_ref[12 + b:13 + b, 32:32 + wide]
        small[7][...] = sg_ref[14 + b:15 + b, 32:32 + 4 * wide]
    for arrive, leave in copies:
        arrive.wait()
        leave.start()
    for _, leave in copies:
        leave.wait()


def settle(big, sg, wide, ups):
    anywhere = pl.BlockSpec(memory_space=pl.ANY)
    inside = pl.BlockSpec(memory_space=pltpu.VMEM)
    row = jax.ShapeDtypeStruct((1, wide), F32)
    small = [row] * 6 + [jax.ShapeDtypeStruct((2, wide), F32), jax.ShapeDtypeStruct((1, ups), F32)]
    outs = pl.pallas_call(
        functools.partial(settle_kernel, wide),
        out_shape=[jax.ShapeDtypeStruct(v.shape, v.dtype) for v in big] + small + small,
        in_specs=[anywhere] * 10 + [inside],
        out_specs=[anywhere] * 10 + [inside] * 16,
        scratch_shapes=[pltpu.VMEM(v.shape, v.dtype) for v in big] + [pltpu.SemaphoreType.DMA((2, 10))],
        name="settle",
    )(*big, sg)
    return outs[:10], (outs[10:18], outs[18:26])


def shards_of(ndp, nmp, inputs, cotangent, mask_bits, *params):
    frame, tube = params[:12], params[12:]
    d = inputs.shape[1]
    rows = inputs.shape[0]
    outer = ndp // INNER
    groups = [[qq * outer + lo for lo in range(outer)] for qq in range(INNER)]

    def joined(values, axis):
        if outer == 1:
            return values
        return lax.all_gather(values, "dp", axis=axis, tiled=True, axis_index_groups=groups)

    matrices = []
    vectors = []
    for block in (frame, tube):
        matrices += [
            joined(block[2].transpose(1, 0, 2), 1),
            joined(block[4], 1),
            joined(block[8], 0),
            joined(block[10].T, 0),
        ]
        vectors += [joined(block[i][None], 1) for i in (0, 1, 5, 6, 7, 11)]
    vectors += [joined(block[3], 1) for block in (frame, tube)]
    vectors += [joined(block[9][None], 1) for block in (frame, tube)]
    wide, ups = vectors[0].shape[1], vectors[-1].shape[1]
    outs = fused((outer, nmp, d, rows), inputs, cotangent, mask_bits[None], matrices, vectors, ndp)
    big, sg = list(outs[:10]), outs[10]
    if outer == 1:
        big, small = settle(big, sg, wide, ups)
    else:
        low = lax.axis_index("dp") % outer
        sg = lax.psum(sg, "dp", axis_index_groups=groups)

        def piece(values, start, size):
            size = size // outer
            return lax.dynamic_slice_in_dim(values, start + low * size, size, 1)

        small = []
        for b in range(2):
            parts = [piece(sg[6 * b + i:6 * b + i + 1], 0, wide) for i in range(6)]
            pair = sg[12 + b, 0:64].reshape(2, 32)
            small.append(parts + [piece(pair, 0, wide), piece(sg[14 + b:15 + b], 32, ups)])
            for i, axis in enumerate((1, 1, 0, 0)):
                at = 2 + 4 * b + i
                big[at] = lax.psum_scatter(
                    big[at], "dp", scatter_dimension=axis, tiled=True, axis_index_groups=groups
                )
    results = []
    for b in range(2):
        inw, outw, up, down = big[2 + 4 * b:6 + 4 * b]
        rows_ = small[b]
        results += [
            rows_[0].reshape(-1),
            rows_[1].reshape(-1),
            inw.transpose(1, 0, 2),
            rows_[6],
            outw,
            rows_[2].reshape(-1),
            rows_[3].reshape(-1),
            rows_[4].reshape(-1),
            up,
            rows_[7].reshape(-1),
            down.T,
            rows_[5].reshape(-1),
        ]
    return (big[0], big[1]) + tuple(results)


def solution(mesh):
    rows = P(("dp", "mp"), None)
    small = P(("dp", "mp"))
    block = (
        small,
        small,
        P("dp", None, "mp"),
        P(None, ("mp", "dp")),
        P("mp", "dp"),
        small,
        small,
        small,
        P("dp", "mp"),
        P(("mp", "dp")),
        P("mp", "dp"),
        small,
    )
    return jax.shard_map(
        functools.partial(shards_of, mesh.shape["dp"], mesh.shape["mp"]),
        mesh=mesh,
        in_specs=(rows, rows, small) + block + block,
        out_specs=(rows, rows) + block + block,
        check_vma=False,
    )
```

time: 340 us -> 285 us (0.84)
  Pallas kernels: 311 us -> 284 us
  other arithmetic: 17.2 us -> 0 us
  local copies, waits for them, and re-layouts: 10.8 us -> 0 us
    pallas_call x1 -> x2, Pallas kernels: 311 us -> 284 us  [the longest x1 279 us: fused(): pl.pallas_call(functools.partial(kernel, sizes, len(vectors)), out_shape=...]
    another operation x17 -> x0, other arithmetic: 11.5 us -> none  [the longest x6 4.05 us: shards_of(): vectors = jnp.stack(vectors).astype(BF16)]
    unnamed x20 -> x0, local copies, waits for them, and re-layouts: 5.29 us -> none
    unnamed x5 -> x0, other arithmetic: 3.56 us -> none
where the time goes in v2:
time: 285 us
  Pallas kernels  284 us (100%)
    pallas_call x1, Pallas kernels, fused(): pl.pallas_call(functools.partial(kernel, sizes, len(vectors)), out_shape=...  279 us

profile of v2, /device:TPU:0, one launch (start us, length us, event | category | flops | bytes accessed | tf_op | source)
XLA Modules:
  0.0 284.6 jit_solution(11898164820400604589)
XLA Ops:
  0.7 279.3 %two_blocks.1 = (f32[256,768]{1,0:T(8,128)}, f32[256,768]{1,0:T(8,128)}, f32[3,96,192]{2,1,0:T(8,128)}, f32[192,96]{1,0:T(8,128)}, f32[96,768]{1,0:T(8,128)}, /*...) custom-call(f32[256,768]{1,0:T(8,128)} %refs_0_.1, ...), custom_call_target="tpu_custom_call" | custom-call | tf_op jit(solution)/shard_map/two_blocks/pallas_call | solution.py:930
  280.0 4.5 %settle.1 = (f32[256,768]{1,0:T(8,128)}, f32[256,768]{1,0:T(8,128)}, f32[3,96,192]{2,1,0:T(8,128)}, f32[192,96]{1,0:T(8,128)}, f32[96,768]{1,0:T(8,128)}, /*inde...) custom-call(f32[256,768]{1,0:T(8,128)} %get-tuple-element.63.refs_0_, ...), custom_call_target="tpu_custom_call" | custom-call | tf_op jit(solution)/shard_map/settle/pallas_call | solution.py:983

commit v3 on v2

--- a/solution.py
+++ b/solution.py
@@ -16,11 +16,31 @@
 CLIP = 4096
 EPS = 1e-06
 INNER = 8
-LEAD = 3
-LAG = 3
+CUT_LOW = 256
+CUT_HIGH = 640
+BACK_LOW = 128
+BACK_HIGH = 512
+LAG = 2
 DEPTH = 3
+ORDER = (
+    [(0, 0), (1, 0), (2, 0), (3, 0)]
+    + [(0, 1), (0, 2), (0, 3), (4, 0)]
+    + [(1, 1), (1, 2), (1, 3), (5, 0)]
+    + [(m, k) for m in (2, 3, 4, 5) for k in (1, 2, 3)]
+)
+Z_AT = {3: (1,), 5: (2,), 8: (3,), 12: (4,), 16: (5,)}
+REST_AT = {3: (0,), 4: (1,), 6: (2,), 9: (3,), 13: (4,), 17: (5,)}
+PASS_AT = {3: (0,), 7: (1,), 11: (2,), 14: (3,), 17: (4,), 20: (5,)}
+PASS_REST_AT = {5: (0,), 8: (1,), 12: (2,), 15: (3,), 18: (4,), 21: (5,)}
+NO_THIRD = (0, 1)
 LAG_TWO = 4
 LAG_THREE = 7
+LAG_FOUR = 9
+LAG_JOIN = 12
+TAIL_TWO = {20: (16, 17), 21: (18, 19), 22: (20,), 23: (21,), 24: (22,), 25: (23,), 26: ()}
+TAIL_THREE = {20: (13, 14), 21: (15, 16), 22: (17, 18), 23: (19, 20), 24: (21,), 25: (22,), 26: (23,)}
+TAIL_FOUR = {20: (11, 12), 21: (13, 14), 22: (15, 16), 23: (17, 18), 24: (19, 20), 25: (21,), 26: (22, 23)}
+TAIL_JOIN = {20: (), 21: (11,), 22: (), 23: (15,), 24: (), 25: (), 26: ()}
 F32 = jnp.float32
 BF16 = jnp.bfloat16
 
@@ -125,6 +145,12 @@
     LS,
     zs,
     zr,
+    zcs,
+    zcr,
+    zds,
+    zdr,
+    hcs,
+    hcr,
     h1s,
     h1r,
     h2s,
@@ -144,6 +170,7 @@
     WI,
     WO,
     SM,
+    XC,
     ls,
 ):
     outer, nmp, d, rows = sizes
@@ -164,6 +191,12 @@
     def place(cc, xx, yy):
         return (yy * 4 + xx * 2 + cc) * outer + low
 
+    assert nmp == 4
+    z1, z2, z3 = flip_by(z, 1), flip_by(z, 2), flip_by(z, 3)
+    across = 2 - z // 2
+    inner = jnp.logical_or(z == 1, z == 2)
+    outermost = jnp.logical_not(inner)
+
     to_c = (place(oc, x, y), z)
     to_x = (place(c, ox, y), z)
     to_y = (place(c, x, oy), z)
@@ -248,29 +281,70 @@
     own_shards(0)
     pl.semaphore_wait(barrier, len(greeted))
 
+    part_one, part_two = pl.ds(0, half), pl.ds(half, half)
+    part_ab = pl.ds(CUT_LOW, CUT_HIGH - CUT_LOW)
+    part_a, part_b = pl.ds(CUT_LOW, half - CUT_LOW), pl.ds(half, CUT_HIGH - half)
+    part_c, part_d = pl.ds(0, CUT_LOW), pl.ds(CUT_HIGH, d - CUT_HIGH)
+
+    def sides(m, zz):
+        return W.at[m, zz, y, :, c, :, part_c], W.at[m, zz, :, x, c, :, part_d]
+
+    def sides_size(m, count):
+        return W.at[m, pl.ds(0, count), y, :, c, :, pl.ds(0, CUT_LOW + d - CUT_HIGH)]
+
     def z_start(m):
-        for key in range(1, nmp):
-            ref = W.at[m, z, y, x, c]
-            send(ref, ref, zs.at[m], zr.at[m, z], to_z(flip_by(z, key)))
+        ref = W.at[m, z, y, x, c, :, part_ab]
+        for zz in (z1, across):
+            send(ref, ref, zs.at[m], zr.at[m, z], to_z(zz))
+
+    def z_pass(m):
+        @pl.when(inner)
+        def _():
+            for zz in (z3, z2):
+                ref = W.at[m, zz, y, x, c, :, part_ab]
+                got(ref, zr.at[m, zz])
+                send(ref, ref, zs.at[m], zr.at[m, zz], to_z(z1))
+
+    def z_rest(m):
+        for ref in sides(m, z):
+            for zz in (z1, across):
+                send(ref, ref, zcs.at[m], zcr.at[m, z], to_z(zz))
+
+    def z_pass_rest(m):
+        @pl.when(inner)
+        def _():
+            for zz in (z3, z2):
+                got(sides_size(m, 1), zcr.at[m, zz])
+                for ref in sides(m, zz):
+                    send(ref, ref, zcs.at[m], zcr.at[m, zz], to_z(z1))
+
+    def arrived(k, ref, sem):
+        if k == 1:
+            got(ref, sem)
+        elif k > 1:
+            pl.when(outermost)(lambda: got(ref, sem))
 
     def g1(m, k):
         zz = flip_by(z, k)
-        if k:
-            got(W.at[m, zz, y, x, c], zr.at[m, zz])
+        arrived(k, W.at[m, zz, y, x, c, :, part_ab], zr.at[m, zz])
         t = m * nmp + k
-        left = W.at[m, zz, y, x, c, :, pl.ds(0, half)]
-        right = W.at[m, zz, y, x, c, :, pl.ds(half, half)]
-        send(left, left, h1s.at[m], h1r.at[t], to_x)
-        send(right, right, h1s.at[m], h1r.at[t], to_y)
+        one = W.at[m, zz, y, x, c, :, part_a if k else part_one]
+        two = W.at[m, zz, y, x, c, :, part_b if k else part_two]
+        send(one, one, h1s.at[m], h1r.at[t], to_x)
+        send(two, two, h1s.at[m], h1r.at[t], to_y)
 
     def g2(m, k):
         zz = flip_by(z, k)
         t = m * nmp + k
-        got(W.at[m, zz, oy, ox, c], h1r.at[t])
-        left = W.at[m, zz, y, :, c, :, pl.ds(0, half)]
-        right = W.at[m, zz, :, x, c, :, pl.ds(half, half)]
-        send(left, left, h2s.at[m], h2r.at[t], to_y)
-        send(right, right, h2s.at[m], h2r.at[t], to_x)
+        if k:
+            got(W.at[m, zz, oy, ox, c, :, part_ab], h1r.at[t])
+        else:
+            got(W.at[m, zz, oy, ox, c], h1r.at[t])
+        arrived(k, sides_size(m, 1), zcr.at[m, zz])
+        one = W.at[m, zz, y, :, c, :, part_one]
+        two = W.at[m, zz, :, x, c, :, part_two]
+        send(one, one, h2s.at[m], h2r.at[t], to_y)
+        send(two, two, h2s.at[m], h2r.at[t], to_x)
 
     def g3(m, k):
         zz = flip_by(z, k)
@@ -285,43 +359,42 @@
         got(W.at[m, zz, :, :, oc], cr.at[t])
 
     def g_done(m):
-        sent(W.at[m, pl.ds(0, nmp - 1), y, x, c], zs.at[m])
-        sent(W.at[m, :, y, x, c], h1s.at[m])
+        for number, which in ((2, outermost), (4, inner)):
+
+            @pl.when(which)
+            def _(number=number):
+                sent(W.at[m, pl.ds(0, number), y, x, c, :, part_ab], zs.at[m])
+                sent(sides_size(m, number), zcs.at[m])
+
+        sent(W.at[m, pl.ds(0, nmp - 1), y, x, c, :, part_ab], h1s.at[m])
+        sent(W.at[m, z, y, x, c], h1s.at[m])
         sent(W.at[m, :, y, :, c], h2s.at[m])
         sent(W.at[m, :, :, :, c], cs.at[m])
 
     total = 6 * nmp
 
-    def advance(t, base=0):
-        def ranged(s, stage):
-            if s < 0:
-                return
-            m, k = s, 0
-            if s >= LEAD:
-                m, k = (s - LEAD) // nmp, (s - LEAD) % nmp
-                if k == 0:
-                    m += LEAD
-            if m < 3 or (m < 6 and isinstance(base, int)):
-                stage(base + m, k)
-            elif m < 6:
-                pl.when(base == 0)(lambda: stage(m, k))
-
-        def first(m, k):
-            if k == 1:
-                if isinstance(m, int):
-                    if m + 1 < 6:
-                        z_start(m + 1)
-                else:
-                    pl.when(m + 1 < 6)(lambda: z_start(m + 1))
-            g1(m, k)
-
-        ranged(t - LAG, g2)
-        ranged(t, first)
-        ranged(t - LAG - DEPTH, g3)
-        ranged(t - LAG - DEPTH - 1, g4)
-
-    def complete(j):
-        return nmp * (j + 1) + LEAD + LAG + DEPTH
+    def advance(t):
+        def at(s, stage):
+            if 0 <= s < total:
+                stage(*ORDER[s])
+
+        at(t - LAG, g2)
+        for m in REST_AT.get(t, ()):
+            z_rest(m)
+        for table, stage in ((Z_AT, z_start), (PASS_AT, z_pass), (PASS_REST_AT, z_pass_rest)):
+            for m in table.get(t, ()):
+                stage(m)
+        at(t, g1)
+        at(t - LAG - DEPTH, g3)
+        at(t - LAG - DEPTH - 1, g4)
+
+    def here(m, k=None):
+        keys = [k] if k is not None else range(nmp)
+        return max(ORDER.index((m, key)) for key in keys) + LAG + DEPTH + 1
+
+    back_a, back_b = pl.ds(BACK_LOW, half - BACK_LOW), pl.ds(half, BACK_HIGH - half)
+    back_ab = pl.ds(BACK_LOW, BACK_HIGH - BACK_LOW)
+    back_c, back_d = pl.ds(0, BACK_LOW), pl.ds(BACK_HIGH, d - BACK_HIGH)
 
     def release(m):
         g_done(m)
@@ -331,63 +404,139 @@
     def may_send(m):
         pl.semaphore_wait(free.at[m], nmp + 1)
 
+    def z_first(m, k, ref, dst, s_sem, r_sem):
+        @pl.when(jnp.logical_and(k != z, jnp.logical_or(outermost, k == z1)))
+        def _():
+            slot = jnp.where(k == z1, z, jnp.where(k == z3, k, z1))
+            send(ref, dst(slot), s_sem.at[m], r_sem.at[m, slot], to_z(z1))
+
+    def z_second(m, k, ref, dst, s_sem, r_sem):
+        @pl.when(jnp.logical_and(inner, jnp.logical_or(k == z2, k == z3)))
+        def _():
+            slot = jnp.where(k == z2, k, z)
+            got(dst(slot), r_sem.at[m, slot])
+            add_to(ref, dst(slot))
+            send(ref, dst(z), s_sem.at[m], r_sem.at[m, z], to_z(k))
+
+    def chunk_refs(m, k, part):
+        return (
+            W.at[m, k, y, x, c, :, part],
+            lambda slot: W.at[m, slot, oy, ox, oc, :, part],
+            zs,
+            zr,
+        )
+
+    def third_refs(m, k):
+        return (
+            W.at[m, k, :, x, c, :, back_c],
+            lambda slot: W.at[m, slot, :, ox, oc, :, back_c],
+            zcs,
+            zcr,
+        )
+
+    def fourth_refs(m, k):
+        return (
+            W.at[m, k, y, :, c, :, back_d],
+            lambda slot: W.at[m, slot, oy, :, oc, :, back_d],
+            zds,
+            zdr,
+        )
+
     def r1(m, k):
         t = m * nmp + k
         send(
-            W.at[m, k, :, ox, c, :, pl.ds(0, half)],
-            W.at[m, k, :, ox, oc, :, pl.ds(0, half)],
+            W.at[m, k, :, ox, c, :, part_one],
+            W.at[m, k, :, ox, oc, :, part_one],
             h2s.at[m],
             h2r.at[t],
             to_x,
         )
         send(
-            W.at[m, k, oy, :, c, :, pl.ds(half, half)],
-            W.at[m, k, oy, :, oc, :, pl.ds(half, half)],
+            W.at[m, k, oy, :, c, :, part_two],
+            W.at[m, k, oy, :, oc, :, part_two],
             h2s.at[m],
             h2r.at[t],
             to_y,
         )
 
+    def either(m, whole, split):
+        if isinstance(m, int):
+            (whole if m in NO_THIRD else split)()
+            return
+        chosen = False
+        for one in NO_THIRD:
+            chosen = jnp.logical_or(chosen, m == one)
+        pl.when(chosen)(whole)
+        pl.when(jnp.logical_not(chosen))(split)
+
     def add_to(dst, src):
         dst[...] = (dst[...].astype(F32) + src[...].astype(F32)).astype(BF16)
 
     def r2(m, k):
         t = m * nmp + k
         got(W.at[m, k, y, :, oc], h2r.at[t])
-        add_to(W.at[m, k, :, x, c, :, pl.ds(0, half)], W.at[m, k, :, x, oc, :, pl.ds(0, half)])
+        add_to(W.at[m, k, :, x, c, :, part_one], W.at[m, k, :, x, oc, :, part_one])
+        add_to(W.at[m, k, y, :, c, :, part_two], W.at[m, k, y, :, oc, :, part_two])
+
+        def second(one, two):
+            send(W.at[m, k, oy, x, c, :, one], W.at[m, k, oy, ox, oc, :, one], h1s.at[m], h1r.at[t], to_y)
+            send(W.at[m, k, y, ox, c, :, two], W.at[m, k, oy, ox, oc, :, two], h1s.at[m], h1r.at[t], to_x)
+
+        def split():
+            second(back_a, back_b)
+            z_first(m, k, *third_refs(m, k))
+            z_first(m, k, *fourth_refs(m, k))
+
+        either(m, lambda: second(part_one, part_two), split)
+
+    def r3(m, k):
+        t = m * nmp + k
+
+        def last(part, one, two):
+            got(W.at[m, k, y, x, oc, :, part], h1r.at[t])
+            add_to(W.at[m, k, y, x, c, :, one], W.at[m, k, y, ox, oc, :, one])
+            add_to(W.at[m, k, y, x, c, :, two], W.at[m, k, oy, x, oc, :, two])
+            z_first(m, k, *chunk_refs(m, k, part))
+
+        either(m, lambda: last(pl.ds(0, d), part_one, part_two), lambda: last(back_ab, back_a, back_b))
+
+    def r3_more(m, k):
+        def split():
+            z_second(m, k, *third_refs(m, k))
+            z_second(m, k, *fourth_refs(m, k))
+            z_second(m, k, *chunk_refs(m, k, back_ab))
+
+        either(m, lambda: z_second(m, k, *chunk_refs(m, k, pl.ds(0, d))), split)
+
+    def join(m):
+        for refs, sem in ((third_refs, zcr), (fourth_refs, zdr)):
+            own, slots = refs(m, z)[:2]
+            mine = own[...].astype(F32)
+            for zz in (z1, across):
+                got(slots(zz), sem.at[m, zz])
+                mine = mine + slots(zz)[...].astype(F32)
+            own[...] = mine.astype(BF16)
+        send(W.at[m, z, oy, x, c, :, back_c], XC.at[m, :, pl.ds(0, BACK_LOW)], hcs.at[m], hcr.at[m], to_y)
         send(
-            W.at[m, k, oy, x, c, :, pl.ds(0, half)],
-            W.at[m, k, oy, ox, oc, :, pl.ds(0, half)],
-            h1s.at[m],
-            h1r.at[t],
-            to_y,
-        )
-        add_to(W.at[m, k, y, :, c, :, pl.ds(half, half)], W.at[m, k, y, :, oc, :, pl.ds(half, half)])
-        send(
-            W.at[m, k, y, ox, c, :, pl.ds(half, half)],
-            W.at[m, k, oy, ox, oc, :, pl.ds(half, half)],
-            h1s.at[m],
-            h1r.at[t],
+            W.at[m, z, y, ox, c, :, back_d],
+            XC.at[m, :, pl.ds(BACK_LOW, d - BACK_HIGH)],
+            hcs.at[m],
+            hcr.at[m],
             to_x,
         )
 
-    def r3(m, k):
-        t = m * nmp + k
-        got(W.at[m, k, y, x, oc], h1r.at[t])
-        add_to(W.at[m, k, y, x, c, :, pl.ds(0, half)], W.at[m, k, y, ox, oc, :, pl.ds(0, half)])
-        add_to(W.at[m, k, y, x, c, :, pl.ds(half, half)], W.at[m, k, oy, x, oc, :, pl.ds(half, half)])
-
-        @pl.when(k != z)
-        def _():
-            send(W.at[m, k, y, x, c], W.at[m, z, oy, ox, oc], zs.at[m], zr.at[m, z], to_z(k))
-
     def r4(m):
-        sum_ = W[m, z, y, x, c].astype(F32)
-        for key in range(1, nmp):
-            zz = flip_by(z, key)
-            src = W.at[m, zz, oy, ox, oc]
+        part = pl.ds(0, d) if m in NO_THIRD else back_ab
+        sum_ = W[m, z, y, x, c, :, part].astype(F32)
+        for zz in (z1, across):
+            src = W.at[m, zz, oy, ox, oc, :, part]
             got(src, zr.at[m, zz])
             sum_ = sum_ + src[...].astype(F32)
+        if m not in NO_THIRD:
+            got(XC.at[m], hcr.at[m])
+            low_part = W[m, z, y, x, c, :, back_c].astype(F32) + XC[m, :, 0:BACK_LOW].astype(F32)
+            high_part = W[m, z, y, x, c, :, back_d].astype(F32) + XC[m, :, BACK_LOW:].astype(F32)
+            sum_ = jnp.concatenate([low_part, sum_, high_part], axis=1)
         b, j = m // 3, m % 3
         if j == 0:
             WI[b, 0] = sum_[:, 0:third]
@@ -405,32 +554,55 @@
         return keep(src, grads_out[b][i], 4 * b + i)
 
     def r_done(m):
-        sent(W.at[m, pl.ds(0, nmp - 1), y, x, c], zs.at[m])
-        sent(W.at[m, :, y, x, c], h1s.at[m])
+        part = pl.ds(0, d) if m in NO_THIRD else back_ab
+        sent(W.at[m, pl.ds(0, nmp - 1), y, x, c, :, part], zs.at[m])
+        sent(W.at[m, :, y, x, c, :, part], h1s.at[m])
         sent(W.at[m, :, y, :, c], h2s.at[m])
+        if m not in NO_THIRD:
+            sent(W.at[m, pl.ds(0, nmp - 1), y, :, c, :, back_c], zcs.at[m])
+            sent(W.at[m, pl.ds(0, nmp - 1), y, :, c, :, back_d], zds.at[m])
+            sent(XC.at[m], hcs.at[m])
 
     def chunk(k):
         key, out, weight = nmp - 1 - k, 0, 1
+        key = jnp.where(jnp.logical_and(inner, key > 1), 5 - key, key)
         while weight < nmp:
             out = out + weight * ((z // weight + key // weight) % 2)
             weight *= 2
         return out
 
+    def join_any(m, k):
+        if isinstance(m, int):
+            if m not in NO_THIRD:
+                join(m)
+        else:
+            either(m, lambda: None, lambda: join(m))
+
     def retreat(u):
         def at(s, stage):
             stage(5 - s // nmp, chunk(s % nmp))
 
         if isinstance(u, int):
+            for v in TAIL_TWO[u]:
+                at(v, r2)
             if u < total:
                 at(u, r1)
-            if u - LAG_TWO < total:
-                at(u - LAG_TWO, r2)
-            if u - LAG_THREE < total:
-                at(u - LAG_THREE, r3)
+            for v in TAIL_THREE[u]:
+                at(v, r3)
+            for v in TAIL_FOUR[u]:
+                at(v, r3_more)
+            for v in TAIL_JOIN[u]:
+                at(v, join_any)
             return
-        at(u, r1)
-        pl.when(u >= LAG_TWO)(lambda: at(u - LAG_TWO, r2))
-        pl.when(u >= LAG_THREE)(lambda: at(u - LAG_THREE, r3))
+        early = u < total - nmp
+        pl.when(early)(lambda: at(u, r1))
+        pl.when(jnp.logical_and(u >= LAG_TWO, early))(lambda: at(u - LAG_TWO, r2))
+        pl.when(jnp.logical_and(u >= LAG_THREE, early))(lambda: at(u - LAG_THREE, r3))
+        pl.when(jnp.logical_and(u >= LAG_FOUR, early))(lambda: at(u - LAG_FOUR, r3_more))
+        own = (u - LAG_JOIN) % nmp == nmp - 1
+        pl.when(jnp.logical_and(jnp.logical_and(u >= LAG_JOIN, own), early))(lambda: at(u - LAG_JOIN, join_any))
+        for v in range(total - nmp, total):
+            pl.when(u == v)(functools.partial(retreat, v))
 
     def swap_start(i):
         RB[i, pl.ds(me, 1)] = SB[i, pl.ds(me, 1)]
@@ -489,7 +661,7 @@
         for b in range(2):
             BI[b, k] = one[12 + 2 * b:13 + 2 * b] * is_q + one[13 + 2 * b:14 + 2 * b] * is_v
             BU[b, k] = two[b:b + 1]
-    for t in range(5, complete(0) + 1):
+    for t in range(5, here(0) + 1):
         advance(t)
 
     lane2 = lax.broadcasted_iota(jnp.int32, (1, 256), 1)
@@ -537,6 +709,24 @@
 
     def forward(b, _):
         m = 3 * b
+        ends = [(here(3 * i), here(3 * i + 1), here(3 * i + 2)) for i in range(2)]
+        done = [here(0), here(3)]
+
+        def turn(upto):
+            for i in range(2):
+                steps_ = range(done[i] + 1, upto[i] + 1)
+                done[i] = max(done[i], upto[i])
+                if len(steps_):
+                    pl.when(b == i)(lambda steps_=steps_: [advance(t) for t in steps_] and None)
+
+        def one_of(i):
+            return [min(done[0] + 1, ends[0][i]), min(done[1] + 1, ends[1][i])]
+
+        @pl.when(b == 1)
+        def _():
+            swap_wait(1)
+            H[1] = rows_of(RB, 1).astype(F32)
+
         h = H[b]
         unit, _s = unit_rows(h)
         normed = unit * SV[b, 0:1] + SV[b, 1:2]
@@ -544,7 +734,7 @@
         NT[b, 0] = tall_view(normed)
         ACC[...] = h + SV[b, 2:3]
 
-        def attend(k, _):
+        def attend(k):
             packed = (mm(NB[...], flat(W[m, k, :, :, :, :, 0:wide])) + BI[b, k, :, 0:wide]).astype(BF16)
             PK[b, k] = packed
             qs = packed[:, 0:256] * BF16(scale)
@@ -560,11 +750,11 @@
             mixed = mixed.astype(BF16)
             CT[b, k] = mixed
             ACC[...] += mm_t(mixed, flat(W[m, k, :, :, :, :, d - 256:d]))
-            return 0
-
-        lax.fori_loop(0, nmp, attend, 0)
-        for t in range(complete(0) + 1, complete(1) + 1):
-            advance(t, m)
+
+        for k in range(nmp):
+            attend(k)
+            if k % 2 == 1 and k < 4:
+                turn(one_of(1))
         middle = ACC[...]
         M[b] = middle
         unit, _s = unit_rows(middle)
@@ -573,16 +763,6 @@
         NT[b, 1] = tall_view(normed)
         ACC[...] = middle + SV[b, 5:6]
 
-        def expand(k, _):
-            upper = mm(NB[...], flat(W[m + 1, k])) + BU[b, k]
-            cdf = 0.5 + 0.5 * lax.erf(upper * (0.5 ** 0.5))
-            HID[b, k] = (upper * cdf).astype(BF16)
-            density = jnp.exp(-0.5 * upper * upper) * ((2 * np.pi) ** -0.5)
-            GP[b, k] = (cdf + upper * density).astype(BF16)
-            return 0
-
-        lax.fori_loop(0, nmp, expand, 0)
-
         @pl.when(b == 0)
         def _():
             keep(ct_ref, GR, 9).wait()
@@ -590,6 +770,24 @@
             SB[0] = mm(picked, GR[...].astype(BF16)).astype(BF16).reshape(members, rows // members, d)
             swap_start(0)
 
+        turn([ends[0][1], ends[1][1]])
+
+        def expand(k):
+            upper = mm(NB[...], flat(W[m + 1, k])) + BU[b, k]
+            cdf = 0.5 + 0.5 * lax.erf(upper * (0.5 ** 0.5))
+            HID[b, k] = (upper * cdf).astype(BF16)
+            density = jnp.exp(-0.5 * upper * upper) * ((2 * np.pi) ** -0.5)
+            GP[b, k] = (cdf + upper * density).astype(BF16)
+
+        def contract(k):
+            pl.when(b == 1)(lambda: shrink(1, k))
+            ACC[...] += mm_t(HID[b, k], flat(W[m + 2, k]))
+
+        for k in range(nmp):
+            expand(k)
+            if k == 1:
+                turn(one_of(2))
+
         @pl.when(b == 1)
         def _():
             early_to_sibling(1)
@@ -597,24 +795,13 @@
             GR[...] = rows_of(RB, 0).astype(F32)
             take_grad(1)
 
-        def contract(k):
-            pl.when(b == 1)(lambda: shrink(1, k))
-            ACC[...] += mm_t(HID[b, k], flat(W[m + 2, k]))
-
         contract(z)
-        for t in range(complete(1) + 1, complete(2) + 1):
-            advance(t, m)
-            if t > complete(2) - nmp + 1:
-                contract(flip_by(z, t - complete(2) + nmp - 1))
+        for k in range(1, nmp):
+            turn([here(2, k), here(5, k)])
+            contract(flip_by(z, k))
         SB[1 + b] = ACC[...].astype(BF16).reshape(members, rows // members, d)
-        swap_start(1 + b)
-        for t in range(complete(2) + 1, complete(3) + 1):
-            advance(t, m)
-
-        @pl.when(b == 0)
-        def _():
-            swap_wait(1)
-            H[1] = rows_of(RB, 1).astype(F32)
+        pl.when(b == 0)(lambda: swap_start(1))
+        turn([here(3), done[1]])
         return 0
 
     lax.fori_loop(0, 2, forward, 0)
@@ -678,7 +865,7 @@
             return 0
 
         lax.fori_loop(0, nmp, down_grad, 0)
-        pl.when(step == 1)(lambda: r4(5))
+        pl.when(step == 1)(lambda: swap_start(2))
         ACC[...] = jnp.zeros_like(ACC)
 
         def spread_up(k, _):
@@ -699,7 +886,7 @@
             return 0
 
         lax.fori_loop(0, nmp, up_grad, 0)
-        pl.when(step == 1)(lambda: r4(4))
+        pl.when(step == 1)(lambda: r4(5))
         back, gain_grad, bias_grad = norm_back(ACC[...], M[b], SV[b, 3:4])
         SGR[pl.ds(row + 3, 1)] = gain_grad
         SGR[pl.ds(row + 4, 1)] = bias_grad
@@ -783,7 +970,7 @@
         def _():
             pl.semaphore_signal(free_c, inc=1, device_id=to_c, device_id_type=MESH)
 
-        pl.when(step == 1)(lambda: r4(3))
+        pl.when(step == 1)(lambda: r4(4))
 
         @pl.when(step == 0)
         def _():
@@ -793,13 +980,15 @@
 
     lax.fori_loop(0, 2, backward, 0)
 
+    ACC[...] = exact(swap.astype(F32), GR[...], ((1,), (0,)))
+    keep(ACC, ig_ref, 9).start()
     swap_wait(2)
     H[1] = mm(swap, rows_of(RB, 2))
     keep(H.at[1], out_ref, 8).start()
-    ACC[...] = exact(swap.astype(F32), GR[...], ((1,), (0,)))
-    keep(ACC, ig_ref, 9).start()
-    for u in range(total, total + LAG_THREE):
-        retreat(u)
+    for u in sorted(TAIL_TWO):
+        if u >= total:
+            retreat(u)
+    r4(3)
     r4(2)
     got(XR.at[pl.ds(1, nmp * per - 1)], rr.at[0])
     sg_ref[...] = XS[z, q] + jnp.sum(XR[1:nmp * per], axis=0)
@@ -898,6 +1087,12 @@
         dma((6,)),
         dma((6, nmp)),
         dma((6,)),
+        dma((6, nmp)),
+        dma((6,)),
+        dma((6, nmp)),
+        dma((6,)),
+        dma((6,)),
+        dma((6,)),
         dma((steps,)),
         dma((6,)),
         dma((steps,)),
@@ -916,6 +1111,7 @@
         vmem((2, 3, block, d // nmp), F32),
         vmem((2, d // nmp, block), F32),
         vmem((16, 128), F32),
+        vmem((6, block, d - BACK_HIGH + BACK_LOW), BF16),
         dma((10,)),
     ]
     grads = [
@@ -950,8 +1146,10 @@
 
 
 def settle_kernel(wide, *refs):
-    big, sg_ref, outs = refs[:10], refs[10], refs[11:37]
-    held, sems = refs[37:47], refs[47]
+    big, sg_in, outs = refs[:10], refs[10], refs[11:37]
+    held, sg_ref, sems = refs[37:47], refs[47], refs[48]
+    small_copy = pltpu.make_async_copy(sg_in, sg_ref, sems.at[0, 10])
+    small_copy.start()
     copies = []
     for i in range(10):
         copies.append(
@@ -961,6 +1159,7 @@
             )
         )
         copies[i][0].start()
+    small_copy.wait()
     for b in range(2):
         small = outs[10 + 8 * b:18 + 8 * b]
         for i in range(6):
@@ -983,9 +1182,10 @@
     outs = pl.pallas_call(
         functools.partial(settle_kernel, wide),
         out_shape=[jax.ShapeDtypeStruct(v.shape, v.dtype) for v in big] + small + small,
-        in_specs=[anywhere] * 10 + [inside],
+        in_specs=[anywhere] * 11,
         out_specs=[anywhere] * 10 + [inside] * 16,
-        scratch_shapes=[pltpu.VMEM(v.shape, v.dtype) for v in big] + [pltpu.SemaphoreType.DMA((2, 10))],
+        scratch_shapes=[pltpu.VMEM(v.shape, v.dtype) for v in (*big, sg)]
+        + [pltpu.SemaphoreType.DMA((2, 11))],
         name="settle",
     )(*big, sg)
     return outs[:10], (outs[10:18], outs[18:26])

time: 285 us -> 259 us (0.909)
  Pallas kernels: 284 us -> 258 us
    pallas_call x1, Pallas kernels: 279 us -> 254 us  [fused(): pl.pallas_call(functools.partial(kernel, sizes, len(vectors)), out_shape=...]
where the time goes in v3:
time: 259 us
  Pallas kernels  258 us (100%)
    pallas_call x1, Pallas kernels, fused(): pl.pallas_call(functools.partial(kernel, sizes, len(vectors)), out_shape=...  254 us

profile of v3, /device:TPU:0, one launch (start us, length us, event | category | flops | bytes accessed | tf_op | source)
XLA Modules:
  0.0 258.6 jit_solution(6336466085526932507)
XLA Ops:
  0.7 253.9 %two_blocks.1 = (f32[256,768]{1,0:T(8,128)}, f32[256,768]{1,0:T(8,128)}, f32[3,96,192]{2,1,0:T(8,128)}, f32[192,96]{1,0:T(8,128)}, f32[96,768]{1,0:T(8,128)}, /*...) custom-call(f32[256,768]{1,0:T(8,128)} %refs_0_.1, ...), custom_call_target="tpu_custom_call" | custom-call | tf_op jit(solution)/shard_map/two_blocks/pallas_call | solution.py:1126
  254.6 3.8 %settle.1 = (f32[256,768]{1,0:T(8,128)}, f32[256,768]{1,0:T(8,128)}, f32[3,96,192]{2,1,0:T(8,128)}, f32[192,96]{1,0:T(8,128)}, f32[96,768]{1,0:T(8,128)}, /*inde...) custom-call(f32[256,768]{1,0:T(8,128)} %get-tuple-element.63.refs_0_, ...), custom_call_target="tpu_custom_call" | custom-call | tf_op jit(solution)/shard_map/settle/pallas_call | solution.py:1182

commit v4 on v3

--- a/solution.py
+++ b/solution.py
@@ -24,14 +24,14 @@
 DEPTH = 3
 ORDER = (
     [(0, 0), (1, 0), (2, 0), (3, 0)]
-    + [(0, 1), (0, 2), (0, 3), (4, 0)]
-    + [(1, 1), (1, 2), (1, 3), (5, 0)]
-    + [(m, k) for m in (2, 3, 4, 5) for k in (1, 2, 3)]
+    + [(m, k) for m in (0, 1) for k in (1, 2, 3)]
+    + [(4, 0), (2, 1), (2, 2), (2, 3), (3, 1), (3, 2), (3, 3), (5, 0)]
+    + [(m, k) for m in (4, 5) for k in (1, 2, 3)]
 )
-Z_AT = {3: (1,), 5: (2,), 8: (3,), 12: (4,), 16: (5,)}
-REST_AT = {3: (0,), 4: (1,), 6: (2,), 9: (3,), 13: (4,), 17: (5,)}
-PASS_AT = {3: (0,), 7: (1,), 11: (2,), 14: (3,), 17: (4,), 20: (5,)}
-PASS_REST_AT = {5: (0,), 8: (1,), 12: (2,), 15: (3,), 18: (4,), 21: (5,)}
+Z_AT = {2: (1,), 5: (2,), 8: (3,), 12: (4,), 16: (5,)}
+REST_AT = {2: (0,), 3: (1,), 5: (2,), 10: (3,), 13: (4,), 19: (5,)}
+PASS_AT = {2: (0,), 6: (1,), 10: (2,), 13: (3,), 17: (4,), 20: (5,)}
+PASS_REST_AT = {5: (0,), 8: (1,), 12: (2,), 15: (3,), 19: (4,), 22: (5,)}
 NO_THIRD = (0, 1)
 LAG_TWO = 4
 LAG_THREE = 7
@@ -90,15 +90,19 @@
     count,
     *refs,
 ):
-    x_ref, ct_ref, bits_ref = refs[:3]
+    x_ref, ct_ref = refs[:2]
     matrices = (refs[3:7], refs[7:11])
-    vectors = refs[11:11 + count]
-    swap_ref, tiles_ref, mask_ref, out_ref, ig_ref = refs[11 + count:16 + count]
+    out_ref, ig_ref = refs[14 + count:16 + count]
     grads_out = (refs[16 + count:20 + count], refs[20 + count:24 + count])
     sg_ref = refs[24 + count]
+    sources = (refs[2], *refs[11:14 + count])
+    held = refs[-len(sources) - 1:-1]
+    bits_ref, vectors, (swap_ref, tiles_ref, mask_ref) = held[0], held[1:1 + count], held[1 + count:]
+    sems = refs[-1]
+    loads = [pltpu.make_async_copy(src, dst, sems.at[i]) for i, (src, dst) in enumerate(zip(sources, held))]
     body(
         sizes, x_ref, ct_ref, bits_ref, matrices, vectors, swap_ref, tiles_ref, mask_ref, out_ref, ig_ref,
-        grads_out, sg_ref, *refs[25 + count:]
+        grads_out, sg_ref, loads, *refs[25 + count:-len(sources) - 1]
     )
 
 
@@ -116,6 +120,7 @@
     ig_ref,
     grads_out,
     sg_ref,
+    loads,
     W,
     SG,
     SV,
@@ -244,19 +249,24 @@
             keep(down, M.at[b, pl.ds(block, block)], 4 * b + 3),
         )
 
-    for b in range(2):
-        for copy in matrix_copies(b):
-            copy.start()
-    keep(x_ref, ACC, 8).start()
-    keep(ct_ref, GR, 9).start()
-
     barrier = pltpu.get_barrier_semaphore()
     greeted = [to_peer(key) for key in range(1, nmp * per)]
     if outer > 1:
         greeted += [to_member(flip_by(me, key)) for key in range(1, members)]
     for device in greeted:
         pl.semaphore_signal(barrier, inc=1, device_id=device, device_id_type=MESH)
+    for copy in loads[1:-3]:
+        copy.start()
+    for b in range(2):
+        for copy in matrix_copies(b):
+            copy.start()
+    keep(x_ref, ACC, 8).start()
+    keep(ct_ref, GR, 9).start()
+    for copy in [*loads[-3:], loads[0]]:
+        copy.start()
     SM[...] = jnp.zeros_like(SM)
+    for copy in loads[1:-3]:
+        copy.wait()
     narrow = 0
     for i, ref in enumerate(vectors[:12]):
         narrow = ref.shape[1]
@@ -629,6 +639,8 @@
     got(SG.at[pl.ds(0, nmp - 1), y, x, c], vr.at[0])
     ref = SG.at[:, y, x, c]
     send(ref, ref, vs.at[1], vr.at[1], to_x)
+    for copy in [*loads[-3:], loads[0]]:
+        copy.wait()
     swap = swap_ref[...]
     keep(x_ref, ACC, 8).wait()
     H[0] = exact(swap.astype(F32), ACC[...], ((1,), (0,)))
@@ -687,10 +699,13 @@
     def to_sibling(src, dst, n):
         send(src, dst, ss.at[n], sr.at[n], to_c)
 
+    def norm_to_sibling(b, i):
+        to_sibling(NT.at[b, i, :, :, oc], LS.at[i], 1 + i)
+
     def early_to_sibling(b):
         to_sibling(HID.at[b], HS, 0)
-        to_sibling(NT.at[b, 0, :, :, oc], LS.at[0], 1)
-        to_sibling(NT.at[b, 1, :, :, oc], LS.at[1], 2)
+        for i in range(2):
+            norm_to_sibling(b, i)
         to_sibling(CT.at[b], CS, 3)
 
     def take_grad(b):
@@ -732,6 +747,7 @@
         normed = unit * SV[b, 0:1] + SV[b, 1:2]
         NB[...] = normed.astype(BF16)
         NT[b, 0] = tall_view(normed)
+        pl.when(b == 1)(lambda: norm_to_sibling(1, 0))
         ACC[...] = h + SV[b, 2:3]
 
         def attend(k):
@@ -749,6 +765,7 @@
                 mixed += mm(probs, vv * v_masks[h])
             mixed = mixed.astype(BF16)
             CT[b, k] = mixed
+            pl.when(b == 1)(lambda: to_sibling(CT.at[1, k], CS.at[k], 3))
             ACC[...] += mm_t(mixed, flat(W[m, k, :, :, :, :, d - 256:d]))
 
         for k in range(nmp):
@@ -761,6 +778,7 @@
         normed = unit * SV[b, 3:4] + SV[b, 4:5]
         NB[...] = normed.astype(BF16)
         NT[b, 1] = tall_view(normed)
+        pl.when(b == 1)(lambda: norm_to_sibling(1, 1))
         ACC[...] = middle + SV[b, 5:6]
 
         @pl.when(b == 0)
@@ -778,6 +796,7 @@
             HID[b, k] = (upper * cdf).astype(BF16)
             density = jnp.exp(-0.5 * upper * upper) * ((2 * np.pi) ** -0.5)
             GP[b, k] = (cdf + upper * density).astype(BF16)
+            pl.when(b == 1)(lambda: to_sibling(HID.at[1, k], HS.at[k], 0))
 
         def contract(k):
             pl.when(b == 1)(lambda: shrink(1, k))
@@ -790,7 +809,6 @@
 
         @pl.when(b == 1)
         def _():
-            early_to_sibling(1)
             swap_wait(0)
             GR[...] = rows_of(RB, 0).astype(F32)
             take_grad(1)
@@ -1113,6 +1131,12 @@
         vmem((16, 128), F32),
         vmem((6, block, d - BACK_HIGH + BACK_LOW), BF16),
         dma((10,)),
+        vmem(bits.shape, bits.dtype),
+        *(vmem(v.shape, v.dtype) for v in vectors),
+        vmem((FRAME, FRAME), BF16),
+        vmem(tiles.shape, BF16),
+        vmem(masks.shape, F32),
+        dma((4 + len(vectors),)),
     ]
     grads = [
         jax.ShapeDtypeStruct((3, block, d // nmp), F32),
@@ -1126,7 +1150,7 @@
     return pl.pallas_call(
         functools.partial(kernel, sizes, len(vectors)),
         out_shape=[whole, whole] + grads + grads + [jax.ShapeDtypeStruct((16, 128), F32)],
-        in_specs=[anywhere] * 2 + [inside] + [anywhere] * 8 + [inside] * (len(vectors) + 3),
+        in_specs=[anywhere] * (14 + len(vectors)),
         out_specs=[anywhere] * 10 + [inside],
         scratch_shapes=scratch,
         compiler_params=pltpu.CompilerParams(

time: 259 us -> 256 us (0.988)
  Pallas kernels: 258 us -> 255 us
    pallas_call x1, Pallas kernels: 254 us -> 251 us  [fused(): pl.pallas_call(functools.partial(kernel, sizes, len(vectors)), out_shape=...]
where the time goes in v4:
time: 256 us
  Pallas kernels  255 us (100%)
    pallas_call x1, Pallas kernels, fused(): pl.pallas_call(functools.partial(kernel, sizes, len(vectors)), out_shape=...  251 us

profile of v4, /device:TPU:0, one launch (start us, length us, event | category | flops | bytes accessed | tf_op | source)
XLA Modules:
  0.0 255.5 jit_solution(8752121447388658260)
XLA Ops:
  0.7 250.8 %two_blocks.1 = (f32[256,768]{1,0:T(8,128)}, f32[256,768]{1,0:T(8,128)}, f32[3,96,192]{2,1,0:T(8,128)}, f32[192,96]{1,0:T(8,128)}, f32[96,768]{1,0:T(8,128)}, /*...) custom-call(f32[256,768]{1,0:T(8,128)} %refs_0_.1, ...), custom_call_target="tpu_custom_call" | custom-call | tf_op jit(solution)/shard_map/two_blocks/pallas_call | solution.py:1150
  251.5 3.8 %settle.1 = (f32[256,768]{1,0:T(8,128)}, f32[256,768]{1,0:T(8,128)}, f32[3,96,192]{2,1,0:T(8,128)}, f32[192,96]{1,0:T(8,128)}, f32[96,768]{1,0:T(8,128)}, /*inde...) custom-call(f32[256,768]{1,0:T(8,128)} %get-tuple-element.63.refs_0_, ...), custom_call_target="tpu_custom_call" | custom-call | tf_op jit(solution)/shard_map/settle/pallas_call | solution.py:1206

commit v5 on v4

--- a/solution.py
+++ b/solution.py
@@ -742,6 +742,13 @@
             swap_wait(1)
             H[1] = rows_of(RB, 1).astype(F32)
 
+        @pl.when(b == 0)
+        def _():
+            keep(ct_ref, GR, 9).wait()
+            picked = (swap.astype(F32) * bits_ref[...].astype(F32)).astype(BF16)
+            SB[0] = mm(picked, GR[...].astype(BF16)).astype(BF16).reshape(members, rows // members, d)
+            swap_start(0)
+
         h = H[b]
         unit, _s = unit_rows(h)
         normed = unit * SV[b, 0:1] + SV[b, 1:2]
@@ -780,13 +787,6 @@
         NT[b, 1] = tall_view(normed)
         pl.when(b == 1)(lambda: norm_to_sibling(1, 1))
         ACC[...] = middle + SV[b, 5:6]
-
-        @pl.when(b == 0)
-        def _():
-            keep(ct_ref, GR, 9).wait()
-            picked = (swap.astype(F32) * bits_ref[...].astype(F32)).astype(BF16)
-            SB[0] = mm(picked, GR[...].astype(BF16)).astype(BF16).reshape(members, rows // members, d)
-            swap_start(0)
 
         turn([ends[0][1], ends[1][1]])
 

time: 256 us -> 256 us (level)
  no operation moved by 1% of the time
where the time goes in v5:
time: 256 us; the launch traced here: 255 us
  Pallas kernels  255 us (100%)
    pallas_call x1, Pallas kernels, fused(): pl.pallas_call(functools.partial(kernel, sizes, len(vectors)), out_shape=...  251 us

profile of v5, /device:TPU:0, one launch (start us, length us, event | category | flops | bytes accessed | tf_op | source)
XLA Modules:
  0.0 255.5 jit_solution(11720383527811235756)
XLA Ops:
  0.7 250.8 %two_blocks.1 = (f32[256,768]{1,0:T(8,128)}, f32[256,768]{1,0:T(8,128)}, f32[3,96,192]{2,1,0:T(8,128)}, f32[192,96]{1,0:T(8,128)}, f32[96,768]{1,0:T(8,128)}, /*...) custom-call(f32[256,768]{1,0:T(8,128)} %refs_0_.1, ...), custom_call_target="tpu_custom_call" | custom-call | tf_op jit(solution)/shard_map/two_blocks/pallas_call | solution.py:1150
  251.5 3.8 %settle.1 = (f32[256,768]{1,0:T(8,128)}, f32[256,768]{1,0:T(8,128)}, f32[3,96,192]{2,1,0:T(8,128)}, f32[192,96]{1,0:T(8,128)}, f32[96,768]{1,0:T(8,128)}, /*inde...) custom-call(f32[256,768]{1,0:T(8,128)} %get-tuple-element.63.refs_0_, ...), custom_call_target="tpu_custom_call" | custom-call | tf_op jit(solution)/shard_map/settle/pallas_call | solution.py:1206
